TPU v7x, 128 devices: a whole 4x4x4 slice. The times are simulated.
128 devices in a mesh: row: 8 (over z, core), col: 8 (over x_lo, y), rep: 2 (over x_hi).
Axes of the slice: x: 4 (x_hi: 2, x_lo: 2; x = x_hi * 2 + x_lo), y: 4, z: 4, core: 2. Of those that a mesh axis runs over, the one named last changes fastest.
Arguments:
- pair: bfloat16 [1024, 512, 128], P(('rep', 'row'), 'col'), parts along dimension 0, may hold values from -6 to 6
- length: int32 [2], P('rep'), parts along dimension 0, may hold values from 128 to 512
- ln_in_gain: float32 [128], replicated, may hold values from 0.1 to 1.9
- ln_in_bias: float32 [128], replicated, may hold values from -1.2 to 1.2
- w_left: bfloat16 [128, 256], replicated, may hold values from -0.5 to 0.5
- w_right: bfloat16 [128, 256], replicated, may hold values from -0.5 to 0.5
- w_gate: bfloat16 [128, 128], replicated, may hold values from -0.5 to 0.5
- product_norm_gain: float32 [128], replicated, may hold values from 0.1 to 1.9
- product_norm_bias: float32 [128], replicated, may hold values from -1.2 to 1.2
- w_out: bfloat16 [128, 128], replicated, may hold values from -0.5 to 0.5
- cotangent: bfloat16 [1024, 512, 128], P(('rep', 'row'), 'col'), parts along dimension 0, may hold values from -6 to 6
Outputs:
- updated: bfloat16 [1024, 512, 128], P(('rep', 'row'), 'col'), parts along dimension 0
- d_pair: bfloat16 [1024, 512, 128], P(('rep', 'row'), 'col'), parts along dimension 0
- grad_left: float32 [256, 256], P('rep'), parts along dimension 0
- grad_right: float32 [256, 256], P('rep'), parts along dimension 0
- grad_gate: float32 [256, 128], P('rep'), parts along dimension 0
- grad_out: float32 [256, 128], P('rep'), parts along dimension 0
There are 2 independent parts, one for each index of `rep`. A program takes and returns all parts, laid end to end along the dimension named above; an argument that names none is the same for every part. Nothing has to cross between parts.
Inputs may be any that keep to these rules, and one draw needn't show every extreme that they name: Token i is valid when i < length.
All inputs are finite; a program needn't handle non-finite values.
Results may differ from a plain program's by a relative error of at most 0.02.
Values may be sent and summed in bfloat16 or wider, within the bound.
No kernel may reach another device: no remote copies, remote signals or barrier semaphores. Data moves between devices by JAX's collectives and lax.ppermute only.
A program may use at most 128 MiB of HBM per device.

v0:
```python
import jax
import jax.numpy as jnp
from jax import lax
from jax.sharding import PartitionSpec as P


def apply_layer_norm(values):
    centered = values - jnp.mean(values, axis=-1, keepdims=True)
    inverse = lax.rsqrt(jnp.mean(centered * centered, axis=-1, keepdims=True) + 1e-05)
    return (centered * inverse, inverse)


def layer_norm_backward(grad_hat, normed, inverse):
    return inverse * (
        grad_hat
        - jnp.mean(grad_hat, axis=-1, keepdims=True)
        - normed * jnp.mean(grad_hat * normed, axis=-1, keepdims=True)
    )


def gated_grad(grad_val, mask, projected, sigma, hidden):
    value_part = grad_val * mask * sigma
    gate_part = grad_val * mask * projected[..., :hidden] * sigma * (1.0 - sigma)
    return jnp.concatenate([value_part, gate_part], axis=-1).astype(jnp.bfloat16)


def body(
    pair,
    length,
    ln_in_gain,
    ln_in_bias,
    w_left,
    w_right,
    w_gate,
    product_norm_gain,
    product_norm_bias,
    w_out,
    cotangent,
):
    tile_i, tile_j, chans = pair.shape
    hidden = w_out.shape[0]
    total = tile_j * lax.axis_size("col")
    row_first = lax.axis_index("row") * tile_i
    col_first = lax.axis_index("col") * tile_j
    row_valid = row_first + jnp.arange(tile_i) < length[0]
    col_valid = col_first + jnp.arange(tile_j) < length[0]
    mask = (row_valid[:, None] & col_valid[None, :]).astype(jnp.float32)[..., None]
    zhat, inv_in = apply_layer_norm(pair.astype(jnp.float32))
    normed = (zhat * ln_in_gain + ln_in_bias).astype(jnp.bfloat16)
    flat = normed.reshape(-1, chans)
    left = jnp.dot(flat, w_left, preferred_element_type=jnp.float32).reshape(
        tile_i, tile_j, 2 * hidden
    )
    right = jnp.dot(flat, w_right, preferred_element_type=jnp.float32).reshape(
        tile_i, tile_j, 2 * hidden
    )
    sig_left = jax.nn.sigmoid(left[..., hidden:])
    sig_right = jax.nn.sigmoid(right[..., hidden:])
    a_val = (mask * sig_left * left[..., :hidden]).astype(jnp.bfloat16)
    b_val = (mask * sig_right * right[..., :hidden]).astype(jnp.bfloat16)
    gate = jax.nn.sigmoid(
        jnp.dot(flat, w_gate, preferred_element_type=jnp.float32).reshape(tile_i, tile_j, chans)
    )
    right_rows = lax.all_gather(b_val, "row", axis=0, tiled=True)
    piece = right_rows
    product_flip = lax.psum_scatter(
        jnp.einsum("ikc,jkc->jic", a_val, piece, preferred_element_type=jnp.float32).astype(
            jnp.bfloat16
        ),
        "col",
        scatter_dimension=0,
        tiled=True,
    ).astype(jnp.float32)
    triangle_product = jnp.transpose(product_flip, (1, 0, 2))
    standardized_input, inverse_output_spread = apply_layer_norm(triangle_product)
    output_result = (standardized_input * product_norm_gain + product_norm_bias).astype(
        jnp.bfloat16
    )
    y_flat = output_result.reshape(-1, hidden)
    proj = jnp.dot(y_flat, w_out, preferred_element_type=jnp.float32).reshape(tile_i, tile_j, chans)
    updated = (gate * proj).astype(jnp.bfloat16)
    upstream = cotangent.astype(jnp.float32)
    d_proj = (upstream * gate).astype(jnp.bfloat16)
    d_gpre = (upstream * proj * gate * (1.0 - gate)).astype(jnp.bfloat16)
    d_proj_flat = d_proj.reshape(-1, chans)
    output_gradient = jnp.dot(d_proj_flat, w_out.T, preferred_element_type=jnp.float32).reshape(
        tile_i, tile_j, hidden
    )
    product_gradient = layer_norm_backward(
        output_gradient * product_norm_gain, standardized_input, inverse_output_spread
    ).astype(jnp.bfloat16)
    grad_rows = lax.all_gather(product_gradient, "col", axis=1, tiled=True)
    d_a = jnp.einsum("ijc,jkc->ikc", grad_rows, right_rows, preferred_element_type=jnp.float32)
    piece = grad_rows
    d_b = lax.psum_scatter(
        jnp.einsum("ijc,ikc->jkc", piece, a_val, preferred_element_type=jnp.float32).astype(
            jnp.bfloat16
        ),
        "row",
        scatter_dimension=0,
        tiled=True,
    ).astype(jnp.float32)
    d_left = gated_grad(d_a, mask, left, sig_left, hidden)
    d_right = gated_grad(d_b, mask, right, sig_right, hidden)
    d_left_flat = d_left.reshape(-1, 2 * hidden)
    d_right_flat = d_right.reshape(-1, 2 * hidden)
    d_gpre_flat = d_gpre.reshape(-1, chans)
    d_zn = (
        jnp.dot(d_left_flat, w_left.T, preferred_element_type=jnp.float32)
        + jnp.dot(d_right_flat, w_right.T, preferred_element_type=jnp.float32)
        + jnp.dot(d_gpre_flat, w_gate.T, preferred_element_type=jnp.float32)
    ).reshape(tile_i, tile_j, chans)
    d_pair = layer_norm_backward(d_zn * ln_in_gain, zhat, inv_in).astype(jnp.bfloat16)
    term_left = jnp.dot(flat.T, d_left_flat, preferred_element_type=jnp.float32)
    term_right = jnp.dot(flat.T, d_right_flat, preferred_element_type=jnp.float32)
    term_gate = jnp.dot(flat.T, d_gpre_flat, preferred_element_type=jnp.float32)
    term_out = jnp.dot(y_flat.T, d_proj_flat, preferred_element_type=jnp.float32)
    sum_left, sum_right, sum_gate, sum_out = lax.psum(
        (term_left, term_right, term_gate, term_out), ("row", "col")
    )
    scale = 1.0 / total
    return (updated, d_pair, sum_left * scale, sum_right * scale, sum_gate * scale, sum_out * scale)


def solution(mesh):
    in_specs = (
        P(("rep", "row"), "col", None),
        P("rep"),
        P(),
        P(),
        P(),
        P(),
        P(),
        P(),
        P(),
        P(),
        P(("rep", "row"), "col", None),
    )
    out_specs = (
        P(("rep", "row"), "col", None),
        P(("rep", "row"), "col", None),
        P("rep", None),
        P("rep", None),
        P("rep", None),
        P("rep", None),
    )
    return jax.shard_map(body, mesh=mesh, in_specs=in_specs, out_specs=out_specs, check_vma=False)
```

profile of v0, /device:TPU:1, one launch (start us, length us, event | category | flops | bytes accessed | tf_op | source)
XLA Modules:
  0.0 951.9 jit_solution(4344079066451321152)
XLA Ops:
  11.6 3.3 fusion.60
  15.0 3.4 fusion.58
  19.1 5.0 multiply_convert_fusion.5
  24.1 4.7 copy.34
  28.9 48.9 %all-gather.3.cloned.1.call-done = bf16[512,64,128]{2,1,0:T(8,128)(2,1)} async-done(((bf16[64,64,128]{2,1,0:T(8,128)(2,1)}), bf16[512,64,128]{2,1,0:T(8,128)(2,1)}) %all-gather.3.cloned.1.call-update) | async-done | bytes 8388624 | tf_op jit(solution)/shard_map/all_gather | solution.py:64
  77.8 13.5 %copy.31 = bf16[512,64,128]{0,1,2:T(8,128)(2,1)} copy(bf16[512,64,128]{2,1,0:T(8,128)(2,1)} %all-gather.3.cloned.1.call-done) | data formatting | bytes 16777216 | tf_op jit(solution)/shard_map/all_gather | solution.py:64
  91.3 6.8 convert_bitcast_fusion.1
  98.1 13.7 %copy.28 = bf16[512,64,128]{2,1,0:T(8,128)(2,1)} copy(bf16[512,64,128]{0,1,2:T(8,128)(2,1)} %convert_bitcast_fusion.1) | data formatting | bytes 16777216 | tf_op jit(solution)/shard_map/convert_element_type | solution.py:67
  112.1 92.2 %reduce-scatter.3.cloned.1.call-done = bf16[64,64,128]{2,1,0:T(8,128)(2,1)} async-done(((bf16[512,64,128]{2,1,0:T(8,128)(2,1)}), bf16[64,64,128]{2,1,0:T(8,128)(2,1)}) %reduce-scatter.3.cloned.1.call-update) | async-done | bytes 1048592 | tf_op jit(solution)/shard_map/reduce_scatter | solution.py:66
  206.5 2.5 fusion.48
  210.4 3.1 fusion.15
  213.5 3.6 multiply_reduce_fusion.1
  217.1 3.3 fusion.47
  222.2 90.8 %all-gather.5.cloned.1.call-done = bf16[64,512,128]{2,0,1:T(8,128)(2,1)} async-done(((bf16[64,64,128]{2,0,1:T(8,128)(2,1)}), bf16[64,512,128]{2,0,1:T(8,128)(2,1)}) %all-gather.5.cloned.1.call-update) | async-done | bytes 8388624 | tf_op jit(solution)/shard_map/all_gather | solution.py:92
  313.0 13.6 %copy.32 = bf16[64,512,128]{1,0,2:T(8,128)(2,1)} copy(bf16[64,512,128]{2,0,1:T(8,128)(2,1)} %all-gather.5.cloned.1.call-done) | data formatting | bytes 16777216 | tf_op jit(solution)/shard_map/all_gather | solution.py:92
  326.6 8.9 fusion.79
  335.5 13.6 %copy.36 = bf16[128,64,512]{0,1,2:T(8,128)(2,1)} copy(bf16[128,64,512]{2,1,0:T(8,128)(2,1)} %fusion.79) | data formatting | bytes 16777216 | tf_op jit(solution)/shard_map/ijc,ikc->jkc/dot_general | solution.py:96
  352.6 2.9 convolution_bitcast_fusion
  355.5 10.9 %fusion.78 = f32[128,64,64]{2,1,0:T(8,128)} fusion(bf16[512,64,128]{0,1,2:T(8,128)(2,1)} %copy.31, bf16[64,512,128]{1,0,2:T(8,128)(2,1)} %copy.32), kind=kOutput, calls=%fused_computation.105 | convolution fusion | flops 536870912 | bytes 18874368 | tf_op jit(solution)/shard_map/ijc,jkc->ikc/dot_general | solution.py:93
  366.3 4.5 copy.33
  370.9 29.1 %reduce-scatter.5.cloned.1.call-done = bf16[64,64,128]{2,1,0:T(8,128)(2,1)} async-done(((bf16[512,64,128]{2,1,0:T(8,128)(2,1)}), bf16[64,64,128]{2,1,0:T(8,128)(2,1)}) %reduce-scatter.5.cloned.1.call-update) | async-done | bytes 1048592 | tf_op jit(solution)/shard_map/reduce_scatter | solution.py:95
  400.0 4.8 multiply_convert_fusion.1
  415.8 3.2 fusion.10
  419.1 520.2 %all-reduce.3.cloned.1.call-done = (f32[128,256]{1,0:T(8,128)}, f32[128,256]{1,0:T(8,128)}, f32[128,128]{1,0:T(8,128)}, f32[128,128]{1,0:T(8,128)}) async-done(((f32[128,256]{1,0:T(8,128)}, f32[128,256]{1,0:T(8,128)}, f32[128,128]{1,0:T(8,128)}, f32[128,128]{1,0:T(8,128)}), (f32[128,256]{1,0:T(8,128)}, f32[128,256]{1,0:T(8,128)}, f32[128,128]{1,0:T(8,128)}, ...) | async-done | bytes 393232 | tf_op jit(solution)/shard_map/psum | solution.py:118
  (83 shorter events, 30.5 us)
Async XLA Ops:
  7.2 7.8 copy-start
  7.2 4.4 copy-start.1
  7.2 4.4 copy-start.19
  7.2 4.4 copy-start.21
  7.2 4.4 copy-start.16
  7.2 70.6 %all-gather.3.cloned.1.call-start = ((), (), s32[]{:S(2)}) async-start(), calls=%async_computation.2 | async-start | bytes 9437184 | tf_op jit(solution)/shard_map/all_gather | solution.py:64
  24.1 180.2 %reduce-scatter.3.cloned.1.call-start = ((), (), s32[]{:S(2)}) async-start(), calls=%async_computation.3 | async-start | bytes 9437184 | tf_op jit(solution)/shard_map/reduce_scatter | solution.py:66
  111.8 97.2 %copy-start.17 = (bf16[128,128]{1,0:T(8,128)(2,1)S(1)}, bf16[128,128]{1,0:T(8,128)(2,1)}, u32[]{:S(2)}) copy-start(bf16[128,128]{1,0:T(8,128)(2,1)} %param.20) | copy-start | bytes 98308
  111.8 97.2 %copy-start.20 = (f32[128]{0:T(128)S(1)}, f32[128]{0:T(128)}, u32[]{:S(2)}) copy-start(f32[128]{0:T(128)} %param.18) | copy-start | bytes 1540
  111.8 97.2 %copy-start.22 = (f32[128]{0:T(128)S(1)}, f32[128]{0:T(128)}, u32[]{:S(2)}) copy-start(f32[128]{0:T(128)} %param.19) | copy-start | bytes 1540
  111.8 201.1 %all-gather.5.cloned.1.call-start = ((), (), s32[]{:S(2)}) async-start(), calls=%async_computation.4 | async-start | bytes 9437184 | tf_op jit(solution)/shard_map/all_gather | solution.py:92
  204.3 4.8 copy-start.2
  206.5 3.8 copy-start.12
  206.5 3.8 copy-start.18
  213.5 3.6 copy-start.10
  222.1 177.9 %reduce-scatter.5.cloned.1.call-start = ((), (), s32[]{:S(2)}) async-start(), calls=%async_computation.5 | async-start | bytes 9437184 | tf_op jit(solution)/shard_map/reduce_scatter | solution.py:95
  349.2 590.1 %all-reduce.3.cloned.1.call-start = ((), (), s32[]{:S(2)}) async-start(), calls=%async_computation.6 | async-start | bytes 786432 | tf_op jit(solution)/shard_map/psum | solution.py:118
  350.4 2.3 copy-start.13
  404.8 2.3 copy-start.4
  404.8 2.3 copy-start.6
  404.9 2.3 copy-start.8
  404.9 2.3 copy-start.9
  409.4 2.4 copy-start.5
  409.4 2.4 copy-start.7
  (4 other events, 7.0 us)
Sparse Core Ops, SparseCore 0:
  24.2 53.5 all-gather.2
  111.9 92.3 reduce-scatter.2
  222.3 90.6 all-gather.4
  349.3 50.7 reduce-scatter.4
  415.9 523.3 all-reduce.2
where the time goes:
time: 955 us; the launch traced here: 952 us
  waiting for transfers between devices  781 us (82%)
  local copies, waits for them, and re-layouts  67 us (7%)
  matrix products  54.8 us (6%)
  other arithmetic  33.3 us (3%)
  between operations  14.8 us (2%)
    psum x1, waiting for transfers between devices, body(): lax.psum((term_left, term_right, term_gate, term_out), ('row', 'col'))  520 us
    reduce_scatter x1, waiting for transfers between devices, body(): lax.psum_scatter(jnp.einsum('ikc,jkc->jic', a_val, piece, preferred_eleme...  92.2 us
    all_gather x1, waiting for transfers between devices, body(): grad_rows = lax.all_gather(product_gradient, 'col', axis=1, tiled=True)  90.8 us
    all_gather x1, waiting for transfers between devices, body(): right_rows = lax.all_gather(b_val, 'row', axis=0, tiled=True)  48.9 us
    reduce_scatter x1, waiting for transfers between devices, body(): lax.psum_scatter(jnp.einsum('ijc,ikc->jkc', piece, a_val, preferred_eleme...  29.1 us
  transfers between devices with their start and end apart: 5, of which 5 were waited for; matrix products, arithmetic and copies ran while one was open for 3% of the time, Pallas kernels for 0%

commit v1 on v0

v1 whole, which is shorter than its diff:
```python
import functools

import jax
import jax.numpy as jnp
from jax import lax
from jax.experimental import pallas as pl
from jax.experimental.pallas import tpu as pltpu
from jax.sharding import PartitionSpec as P

AXES = ("row", "col")
BF = jnp.bfloat16
F32 = jnp.float32
STEP = 16
EPS = 1e-05


def dot(lhs, rhs, left_dim, right_dim):
    return lax.dot_general(
        lhs, rhs, (((left_dim,), (right_dim,)), ((), ())), preferred_element_type=F32
    )


def column(ref):
    return jnp.transpose(jnp.broadcast_to(ref[...], (128, 128)))[:, :1]


def normalize(values):
    centered = values - jnp.mean(values, axis=0, keepdims=True)
    inverse = lax.rsqrt(jnp.mean(centered * centered, axis=0, keepdims=True) + EPS)
    return centered * inverse, inverse


def normalize_backward(grad_hat, normed, inverse):
    return inverse * (
        grad_hat
        - jnp.mean(grad_hat, axis=0, keepdims=True)
        - normed * jnp.mean(grad_hat * normed, axis=0, keepdims=True)
    )


def load_transposed(ref):
    rows, cols, chans = ref.shape
    return jnp.transpose(ref[...].reshape(rows * cols, chans)).astype(F32)


def store_transposed(ref, values):
    rows, cols, chans = ref.shape
    ref[...] = jnp.transpose(values.astype(BF)).reshape(rows, cols, chans)


def low_half(shape):
    return lax.broadcasted_iota(jnp.int32, shape, len(shape) - 1) < 64


def pack(values, scr):
    low = low_half((64, 128))
    for t in range(STEP // 2):
        first = values[:64, t * 128 : (t + 1) * 128]
        second = values[64:, t * 128 : (t + 1) * 128]
        scr[pl.ds(2 * t, 64, stride=STEP), :] = jnp.where(low, first, pltpu.roll(second, 64, 1))
        scr[pl.ds(2 * t + 1, 64, stride=STEP), :] = jnp.where(
            low, pltpu.roll(first, 64, 1), second
        )
    return scr[...].reshape(64, STEP, 128).astype(BF)


def unpack(payload, scr):
    low = low_half((64, 128))
    scr[...] = payload.astype(F32).reshape(64 * STEP, 128)
    tiles = []
    for t in range(STEP // 2):
        even = scr[pl.ds(2 * t, 64, stride=STEP), :]
        odd = scr[pl.ds(2 * t + 1, 64, stride=STEP), :]
        first = jnp.where(low, even, pltpu.roll(odd, 64, 1))
        second = jnp.where(low, pltpu.roll(even, 64, 1), odd)
        tiles.append(jnp.concatenate([first, second], axis=0))
    return jnp.concatenate(tiles, axis=1)


def cell_mask(length_ref):
    cells = lax.broadcasted_iota(jnp.int32, (1, STEP * 64), 1)
    row = lax.axis_index("row") * 64 + pl.program_id(0) * STEP + cells // 64
    col = lax.axis_index("col") * 64 + cells % 64
    length = length_ref[0]
    return ((row < length) & (col < length)).astype(F32)


def operands_kernel(pair, length, gain, bias, w_left, w_right, send, zn_out, scr):
    zhat, _ = normalize(load_transposed(pair))
    zn = (zhat * column(gain) + column(bias)).astype(BF)
    zn_out[...] = zn
    mask = cell_mask(length)
    left = dot(w_left[...], zn, 0, 0)
    send[:, 0] = pack(mask * jax.nn.sigmoid(left[128:]) * left[:128], scr)
    right = dot(w_right[...], zn, 0, 0)
    send[:, 1] = pack(mask * jax.nn.sigmoid(right[128:]) * right[:128], scr)


def factors_kernel(zn, length, w_left, w_right, w_gate, cot, sl, gl, sr, gr, gate, cot_out):
    mask = cell_mask(length)
    gate[...] = jax.nn.sigmoid(dot(w_gate[...], zn[...], 0, 0))
    cot_out[...] = load_transposed(cot)
    for weights, slope, bend in ((w_left, sl, gl), (w_right, sr, gr)):
        value = dot(weights[...], zn[...], 0, 0)
        sigma = jax.nn.sigmoid(value[128:])
        slope[...] = mask * sigma
        bend[...] = mask * value[:128] * sigma * (1.0 - sigma)


def gather_map(got, which, scr):
    for r in range(8):
        for c in range(8):
            scr[r * 64 : (r + 1) * 64, c * 128 : (c + 1) * 128] = got[r * 8 + c, which]


def double_rows(got, which, scr):
    low = low_half((64, 128))
    zero = jnp.zeros((64, 128), BF)
    for r in range(8):
        for c in range(8):
            tile = got[r * 8 + c, which]
            lanes = slice(c * 128, (c + 1) * 128)
            scr[r * 128 : r * 128 + 64, lanes] = jnp.where(low, tile, zero)
            scr[r * 128 + 64 : (r + 1) * 128, lanes] = jnp.where(low, zero, tile)


def product_kernel(got, send, a_scr, b_scr):
    gather_map(got, 0, a_scr)
    double_rows(got, 1, b_scr)
    for n in range(4):
        out = dot(a_scr[...], b_scr[n * 256 : (n + 1) * 256, :], 1, 1).astype(BF)
        for r in range(8):
            for c in range(2):
                send[r * 8 + 2 * n + c] = out[r * 64 : (r + 1) * 64, c * 128 : (c + 1) * 128]


def middle_kernel(
    got, gate_ref, cot, zn, gain_ref, bias_ref, w_out,
    updated, send, dg_out, grad_out, grad_gate, scr,
):
    hat, inverse = normalize(unpack(got[...], scr))
    gain = column(gain_ref)
    y = (hat * gain + column(bias_ref)).astype(BF)
    proj = dot(w_out[...], y, 0, 0)
    gate = gate_ref[...]
    upstream = cot[...]
    d_proj = (upstream * gate).astype(BF)
    d_y = dot(w_out[...], d_proj, 1, 0)
    send[...] = pack(normalize_backward(d_y * gain, hat, inverse), scr)
    store_transposed(updated, gate * proj)
    d_gpre = (upstream * proj * gate * (1.0 - gate)).astype(BF)
    dg_out[...] = d_gpre

    @pl.when(pl.program_id(0) == 0)
    def _():
        grad_out[...] = jnp.zeros((128, 128), F32)
        grad_gate[...] = jnp.zeros((128, 128), F32)

    grad_out[...] += dot(y, d_proj, 1, 1)
    grad_gate[...] += dot(zn[...], d_gpre, 1, 1)


def product_grads_kernel(got, operands, send, a_scr, b_scr, d_scr):
    gather_map(operands, 0, a_scr)
    double_rows(operands, 1, b_scr)
    for r in range(8):
        for c in range(8):
            d_scr[r * 64 : (r + 1) * 64, c * 128 : (c + 1) * 128] = got[r * 8 + c]
    for n in range(4):
        out = dot(d_scr[...], b_scr[:, n * 256 : (n + 1) * 256], 1, 0).astype(BF)
        for r in range(8):
            for c in range(2):
                send[r * 8 + 2 * n + c, 0] = out[r * 64 : (r + 1) * 64, c * 128 : (c + 1) * 128]
    low = low_half((64, 128))
    for m in range(2):
        out = dot(d_scr[:, m * 512 : (m + 1) * 512], a_scr[...], 0, 0)
        for r in range(4):
            for c in range(8):
                lanes = slice(c * 128, (c + 1) * 128)
                send[(m * 4 + r) * 8 + c, 1] = jnp.where(
                    low, out[r * 128 : r * 128 + 64, lanes], out[r * 128 + 64 : (r + 1) * 128, lanes]
                ).astype(BF)


def weights_kernel(got, zn, sl, gl, sr, gr, grad_gate, grad_out, dl_out, dr_out, send, scr, acc):
    step = pl.program_id(0)
    z = zn[...]

    @pl.when(step == 0)
    def _():
        acc[...] = jnp.zeros((128, 512), F32)

    for which, slope, bend, out in ((0, sl, gl, dl_out), (1, sr, gr, dr_out)):
        grad = unpack(got[:, which], scr)
        value = jnp.concatenate([grad * slope[...], grad * bend[...]], axis=0).astype(BF)
        out[...] = value
        acc[:, which * 256 : (which + 1) * 256] += dot(z, value, 1, 1)

    @pl.when(step == pl.num_programs(0) - 1)
    def _():
        for t in range(6):
            if t < 4:
                tile = acc[:, t * 128 : (t + 1) * 128]
            else:
                tile = (grad_gate if t == 4 else grad_out)[...]
            for half in range(2):
                send[pl.ds(2 * t + half, 64, stride=16), :] = tile[half * 64 : (half + 1) * 64]
        for t in range(12, 16):
            send[pl.ds(t, 64, stride=16), :] = jnp.zeros((64, 128), F32)


def pair_kernel(pair, gain, dl, dr, dg, w_left, w_right, w_gate, out):
    zhat, inverse = normalize(load_transposed(pair))
    d_zn = (
        dot(w_left[...], dl[...], 1, 0)
        + dot(w_right[...], dr[...], 1, 0)
        + dot(w_gate[...], dg[...], 1, 0)
    )
    store_transposed(out, normalize_backward(d_zn * column(gain), zhat, inverse))


def sum_kernel(scale, got, send):
    send[...] = jnp.broadcast_to((jnp.sum(got[...], axis=0) * scale)[None], send.shape)


def split_kernel(got, left, right, gate, out):
    for t, (ref, lane) in enumerate(
        ((left, 0), (left, 128), (right, 0), (right, 128), (gate, 0), (out, 0))
    ):
        for half in range(2):
            ref[half * 64 : (half + 1) * 64, lane : lane + 128] = got[
                pl.ds(2 * t + half, 64, stride=16), :
            ]


def call(kernel, grid, in_specs, out_specs, out_shape, scratch=(), cost=(10**9, 10**7)):
    return pl.pallas_call(
        kernel,
        grid=grid,
        in_specs=in_specs,
        out_specs=out_specs,
        out_shape=out_shape,
        scratch_shapes=list(scratch),
        cost_estimate=pl.CostEstimate(flops=cost[0], bytes_accessed=cost[1], transcendentals=0),
        compiler_params=pltpu.CompilerParams(vmem_limit_bytes=48 * 1024 * 1024),
    )


def whole(*shape):
    return pl.BlockSpec(shape, lambda *_: (0,) * len(shape))


def shape(dims, kind):
    return jax.ShapeDtypeStruct(dims, kind)


def exchange(values):
    return lax.all_to_all(values, AXES, 0, 0, tiled=True)


def body(
    pair, length, ln_in_gain, ln_in_bias, w_left, w_right, w_gate,
    product_norm_gain, product_norm_bias, w_out, cotangent,
):
    tile_i, tile_j, chans = pair.shape
    total = tile_j * lax.axis_size("col")
    steps = tile_i // STEP
    cells = tile_i * tile_j
    grid = (steps,)
    gain_in, bias_in = ln_in_gain.reshape(1, 128), ln_in_bias.reshape(1, 128)
    gain_p, bias_p = product_norm_gain.reshape(1, 128), product_norm_bias.reshape(1, 128)

    natural = pl.BlockSpec((STEP, 64, 128), lambda i: (i, 0, 0))
    chan_major = pl.BlockSpec((128, STEP * 64), lambda i: (0, i))
    chan_major2 = pl.BlockSpec((256, STEP * 64), lambda i: (0, i))
    single = pl.BlockSpec((64, STEP, 128), lambda i: (0, i, 0))
    double = pl.BlockSpec((64, 2, STEP, 128), lambda i: (0, 0, i, 0))
    scalar = pl.BlockSpec(memory_space=pltpu.SMEM)
    vec, wide, square = whole(1, 128), whole(128, 256), whole(128, 128)
    swap = pltpu.VMEM((64 * STEP, 128), F32)
    f_cells, b_cells = shape((128, cells), F32), shape((128, cells), BF)

    send, zn = call(
        operands_kernel, grid,
        [natural, scalar, vec, vec, wide, wide],
        [double, chan_major],
        [shape((64, 2, 64, 128), BF), b_cells],
        [swap],
    )(pair, length, gain_in, bias_in, w_left, w_right)
    operands = exchange(send.reshape(64, 128, 128)).reshape(64, 2, 64, 128)

    slope_l, bend_l, slope_r, bend_r, gate, upstream = call(
        factors_kernel, grid,
        [chan_major, scalar, wide, wide, square, natural],
        [chan_major] * 6,
        [f_cells] * 6,
    )(zn, length, w_left, w_right, w_gate, cotangent)

    product = call(
        product_kernel, (1,),
        [whole(64, 2, 64, 128)],
        whole(64, 64, 128),
        shape((64, 64, 128), BF),
        [pltpu.VMEM((512, 1024), BF), pltpu.VMEM((1024, 1024), BF)],
    )(operands)

    updated, send, d_gpre, grad_out, grad_gate = call(
        middle_kernel, grid,
        [single, chan_major, chan_major, chan_major, vec, vec, square],
        [natural, single, chan_major, square, square],
        [shape(pair.shape, BF), shape((64, 64, 128), BF), b_cells]
        + [shape((128, 128), F32)] * 2,
        [swap],
    )(exchange(product), gate, upstream, zn, gain_p, bias_p, w_out)

    send = call(
        product_grads_kernel, (1,),
        [whole(64, 64, 128), whole(64, 2, 64, 128)],
        whole(64, 2, 64, 128),
        shape((64, 2, 64, 128), BF),
        [pltpu.VMEM((512, 1024), BF), pltpu.VMEM((1024, 1024), BF), pltpu.VMEM((512, 1024), BF)],
    )(exchange(send), operands)
    grads = exchange(send.reshape(64, 128, 128)).reshape(64, 2, 64, 128)

    d_left, d_right, terms = call(
        weights_kernel, grid,
        [double] + [chan_major] * 5 + [square] * 2,
        [chan_major2, chan_major2, whole(1024, 128)],
        [shape((256, cells), BF)] * 2 + [shape((1024, 128), F32)],
        [swap, pltpu.VMEM((128, 512), F32)],
    )(grads, zn, slope_l, bend_l, slope_r, bend_r, grad_gate, grad_out)
    shares = exchange(terms.reshape(64, 16, 128))

    d_pair = call(
        pair_kernel, grid,
        [natural, vec, chan_major2, chan_major2, chan_major, wide, wide, square],
        natural,
        shape(pair.shape, BF),
    )(pair, gain_in, d_left, d_right, d_gpre, w_left, w_right, w_gate)

    summed = call(
        functools.partial(sum_kernel, 1.0 / total), (1,),
        [whole(64, 16, 128)], whole(64, 16, 128), shape((64, 16, 128), F32), cost=(10**6, 10**6),
    )(shares)
    sums = call(
        split_kernel, (1,),
        [whole(1024, 128)],
        [wide, wide, square, square],
        [shape((128, 256), F32)] * 2 + [shape((128, 128), F32)] * 2, cost=(10**6, 10**6),
    )(exchange(summed).reshape(1024, 128))
    return (updated, d_pair, *sums)


def solution(mesh):
    in_specs = (
        P(("rep", "row"), "col", None),
        P("rep"),
        P(),
        P(),
        P(),
        P(),
        P(),
        P(),
        P(),
        P(),
        P(("rep", "row"), "col", None),
    )
    out_specs = (
        P(("rep", "row"), "col", None),
        P(("rep", "row"), "col", None),
        P("rep", None),
        P("rep", None),
        P("rep", None),
        P("rep", None),
    )
    return jax.shard_map(body, mesh=mesh, in_specs=in_specs, out_specs=out_specs, check_vma=False)
```

time: 955 us -> 187 us (0.20)
  waiting for transfers between devices: 781 us -> 15.1 us
  blocking collectives: 0 us -> 112 us
  matrix products: 54.8 us -> 0 us
  local copies, waits for them, and re-layouts: 67 us -> 13.9 us
  Pallas kernels: 0 us -> 34.2 us
  other arithmetic: 33.3 us -> 0 us
  between operations: 14.8 us -> 1.45 us
    psum x1 -> x0, waiting for transfers between devices: 520 us -> none  [body(): lax.psum((term_left, term_right, term_gate, term_out), ('row', 'col'))]
    all_gather x2 -> x0, waiting for transfers between devices: 140 us -> none  [the longest x1 90.8 us: body(): grad_rows = lax.all_gather(product_gradient, 'col', axis=1, tiled=True)]
    reduce_scatter x2 -> x0, waiting for transfers between devices: 121 us -> none  [the longest x1 92.2 us: body(): lax.psum_scatter(jnp.einsum('ikc,jkc->jic', a_val, piece, preferred_eleme...]
    all_to_all x0 -> x4, blocking collectives: none -> 112 us  [exchange(): return lax.all_to_all(values, AXES, 0, 0, tiled=True)]
    dot_general x15 -> x0, matrix products: 54.8 us -> none  [the longest x1 10.9 us: body(): jnp.einsum('ijc,jkc->ikc', grad_rows, right_rows, preferred_element_type=...]
    pallas_call x0 -> x9, Pallas kernels: none -> 34.2 us  [the longest x1 7.18 us: body(): call(middle_kernel, grid, [single, chan_major, chan_major, chan_major, ve...]
    all_gather x2 -> x0, local copies, waits for them, and re-layouts: 27.1 us -> none  [the longest x1 13.6 us: body(): grad_rows = lax.all_gather(product_gradient, 'col', axis=1, tiled=True)]
    convert_element_type x3 -> x0, local copies, waits for them, and re-layouts: 20.1 us -> none  [the longest x1 13.7 us: body(): jnp.einsum('ikc,jkc->jic', a_val, piece, preferred_element_type=jnp.float32)]
  transfers between devices with their start and end apart: 5 -> 2, of which waited for: 5 -> 2; matrix products, arithmetic and copies ran while one was open for 3% -> 0% of each run, Pallas kernels for 0% -> 5%
where the time goes in v1:
time: 187 us; the launch traced here: 186 us
  blocking collectives  112 us (60%)
  Pallas kernels  34.2 us (18%)
  waiting for transfers between devices  15.1 us (8%)
  local copies, waits for them, and re-layouts  13.9 us (7%)
  starting transfers between devices  9.64 us (5%)
    all_to_all x4, blocking collectives, exchange(): return lax.all_to_all(values, AXES, 0, 0, tiled=True)  112 us
    all_to_all x2, waiting for transfers between devices, exchange(): return lax.all_to_all(values, AXES, 0, 0, tiled=True)  15.1 us
    unnamed x42, local copies, waits for them, and re-layouts  13.9 us
    all_to_all x2, starting transfers between devices, exchange(): return lax.all_to_all(values, AXES, 0, 0, tiled=True)  9.64 us
    pallas_call x1, Pallas kernels, body(): call(middle_kernel, grid, [single, chan_major, chan_major, chan_major, ve...  7.18 us
    pallas_call x1, Pallas kernels, body(): call(weights_kernel, grid, [double] + [chan_major] * 5 + [square] * 2, [c...  7.03 us
    pallas_call x1, Pallas kernels, body(): call(factors_kernel, grid, [chan_major, scalar, wide, wide, square, natur...  5.17 us
    pallas_call x1, Pallas kernels, body(): call(pair_kernel, grid, [natural, vec, chan_major2, chan_major2, chan_maj...  4.78 us
  transfers between devices with their start and end apart: 2, of which 2 were waited for; matrix products, arithmetic and copies ran while one was open for 0% of the time, Pallas kernels for 5%

profile of v1, /device:TPU:1, one launch (start us, length us, event | category | flops | bytes accessed | tf_op | source)
XLA Modules:
  0.0 185.9 jit_solution(7317913487522461164)
XLA Ops:
  1.3 1.2 copy-done.5
  5.5 4.3 %shard_map.154 = (bf16[64,2,64,128]{3,2,1,0:T(8,128)(2,1)S(1)}, bf16[128,4096]{1,0:T(8,128)(2,1)S(1)}) custom-call(bf16[64,64,128]{2,1,0:T(8,128)(2,1)S(1)} %copy-done.5, s32[1]{0:T(128)S(6)} %copy.17.length, f32[1,128]{1,0:T(1,128)S(1)} %bitcast.18, f32[1,128]{1,0:T(1,128)S(1)} %bitcast.20, bf16[128,256]{1,0:T(8,128)(2,1)S(1)} %copy-done.9, ...), custom_call_target="tpu_custom_call" | custom-call | flops 1000000000 | bytes 10000000 | tf_op jit(solution)/shard_map/pallas_call | solution.py:283
  9.8 39.2 %all_to_all.30 = bf16[64,128,128]{2,1,0:T(8,128)(2,1)S(1)} all-to-all(bf16[64,128,128]{2,1,0:T(8,128)(2,1)S(1)} %bitcast.13), channel_id=1, replica_groups=mesh['row'=8,'col'=8,'rep'=2] {'row','col'}, dimensions={0} | all-to-all | bytes 4194304 | tf_op jit(solution)/shard_map/all_to_all | solution.py:258
  49.0 1.4 shard_map.155
  50.4 1.0 copy-done.4
  51.4 5.2 %all-to-all-start.1 = ((bf16[64,64,128]{2,1,0:T(8,128)(2,1)}), bf16[64,64,128]{2,1,0:T(8,128)(2,1)}, u32[]{:S(2)}, u32[]{:S(2)}) async-start(bf16[64,64,128]{2,1,0:T(8,128)(2,1)} %copy-done.4), calls=%async_computation.1 | async-start | bytes 2097152 | tf_op jit(solution)/shard_map/all_to_all | solution.py:258
  56.7 1.2 copy-done.19
  57.9 5.2 %shard_map.156 = (f32[128,4096]{1,0:T(8,128)S(1)}, f32[128,4096]{1,0:T(8,128)}, f32[128,4096]{1,0:T(8,128)}, f32[128,4096]{1,0:T(8,128)}, f32[128,4096]{1,0:T(8,128)}, /*index=5*/f32[128,4096]{1,0:T(8,128)}) custom-call(bf16[128,4096]{1,0:T(8,128)(2,1)S(1)} %get-tuple-element.27.zn, s32[1]{0:T(128)S(6)} %copy.17.length, bf16[128,256]{1,0:T(8,128)(2,1)S(1)} %copy-done.10, ...), custom_call_target="tpu_custom_call" | custom-call | flops 1000000000 | bytes 10000000 | tf_op jit(solution)/shard_map/pallas_call | solution.py:292
  63.1 1.4 copy-done
  64.5 10.0 %all-to-all-done.1.got = bf16[64,64,128]{2,1,0:T(8,128)(2,1)} async-done(((bf16[64,64,128]{2,1,0:T(8,128)(2,1)}), bf16[64,64,128]{2,1,0:T(8,128)(2,1)}, u32[]{:S(2)}, u32[]{:S(2)}) %all-to-all-start.1) | async-done | bytes 1048608 | tf_op jit(solution)/shard_map/all_to_all | solution.py:258
  74.5 7.2 %shard_map.157 = (bf16[64,64,128]{2,1,0:T(8,128)(2,1)}, bf16[64,64,128]{2,1,0:T(8,128)(2,1)S(1)}, bf16[128,4096]{1,0:T(8,128)(2,1)S(1)}, f32[128,128]{1,0:T(8,128)S(1)}, f32[128,128]{1,0:T(8,128)S(1)}) custom-call(bf16[64,64,128]{2,1,0:T(8,128)(2,1)} %all-to-all-done.1.got, f32[128,4096]{1,0:T(8,128)} %get-tuple-element.28.gate_ref, ...), custom_call_target="tpu_custom_call" | custom-call | flops 1000000000 | bytes 10000000 | tf_op jit(solution)/shard_map/pallas_call | solution.py:307
  81.6 1.0 copy-done.7
  82.6 22.2 %all_to_all.31.got = bf16[64,64,128]{2,1,0:T(8,128)(2,1)S(1)} all-to-all(bf16[64,64,128]{2,1,0:T(8,128)(2,1)S(1)} %get-tuple-element.31), channel_id=1, replica_groups=mesh['row'=8,'col'=8,'rep'=2] {'row','col'}, dimensions={0} | all-to-all | bytes 2097152 | tf_op jit(solution)/shard_map/all_to_all | solution.py:258
  104.8 2.6 %shard_map.158 = bf16[64,2,64,128]{3,2,1,0:T(8,128)(2,1)S(1)} custom-call(bf16[64,64,128]{2,1,0:T(8,128)(2,1)S(1)} %all_to_all.31.got, bf16[64,2,64,128]{3,2,1,0:T(8,128)(2,1)S(1)} %bitcast.11), custom_call_target="tpu_custom_call" | custom-call | flops 1000000000 | bytes 10000000 | tf_op jit(solution)/shard_map/pallas_call | solution.py:316
  107.4 32.8 %all_to_all.32 = bf16[64,128,128]{2,1,0:T(8,128)(2,1)} all-to-all(bf16[64,128,128]{2,1,0:T(8,128)(2,1)S(1)} %bitcast.12), channel_id=1, replica_groups=mesh['row'=8,'col'=8,'rep'=2] {'row','col'}, dimensions={0} | all-to-all | bytes 4194304 | tf_op jit(solution)/shard_map/all_to_all | solution.py:258
  140.2 7.0 %shard_map.159 = (bf16[256,4096]{1,0:T(8,128)(2,1)S(1)}, bf16[256,4096]{1,0:T(8,128)(2,1)S(1)}, f32[1024,128]{1,0:T(8,128)S(1)}) custom-call(bf16[64,2,64,128]{3,2,1,0:T(8,128)(2,1)} %bitcast.21, bf16[128,4096]{1,0:T(8,128)(2,1)S(1)} %get-tuple-element.27.zn, f32[128,4096]{1,0:T(8,128)} %copy-done, f32[128,4096]{1,0:T(8,128)} %get-tuple-element.33.gl, ...), custom_call_target="tpu_custom_call" | custom-call | flops 1000000000 | bytes 10000000 | tf_op jit(solution)/shard_map/pallas_call | solution.py:325
  147.3 1.3 copy-done.1
  148.6 1.3 copy-done.3
  149.9 17.3 %all_to_all.33.got = f32[64,16,128]{2,1,0:T(8,128)S(1)} all-to-all(f32[64,16,128]{2,1,0:T(8,128)S(1)} %bitcast.15), channel_id=1, replica_groups=mesh['row'=8,'col'=8,'rep'=2] {'row','col'}, dimensions={0} | all-to-all | bytes 1048576 | tf_op jit(solution)/shard_map/all_to_all | solution.py:258
  168.1 4.5 %all-to-all-start.5 = ((f32[64,16,128]{2,1,0:T(8,128)}), f32[64,16,128]{2,1,0:T(8,128)S(1)}, u32[]{:S(2)}, u32[]{:S(2)}) async-start(f32[64,16,128]{2,1,0:T(8,128)} %shard_map.161), calls=%async_computation.5 | async-start | bytes 1048576 | tf_op jit(solution)/shard_map/all_to_all | solution.py:258
  172.6 1.2 copy-done.6
  173.8 1.2 copy-done.8
  175.1 4.8 %shard_map.160 = bf16[64,64,128]{2,1,0:T(8,128)(2,1)} custom-call(bf16[64,64,128]{2,1,0:T(8,128)(2,1)S(1)} %copy-done.6, f32[1,128]{1,0:T(1,128)S(1)} %bitcast.19, bf16[256,4096]{1,0:T(8,128)(2,1)S(1)} %copy-done.2, bf16[256,4096]{1,0:T(8,128)(2,1)} %copy-done.3, bf16[128,4096]{1,0:T(8,128)(2,1)S(1)} %copy-done.8, bf16[128,256]{1,0:T(8,128)(2,1)S(1)} %copy-done.10, ...), custom_call_target="tpu_custom_call" | custom-call | flops 1000000000 | bytes 10000000 | tf_op jit(solution)/shard_map/pallas_call | solution.py:334
  179.8 5.2 %all-to-all-done.5 = f32[64,16,128]{2,1,0:T(8,128)S(1)} async-done(((f32[64,16,128]{2,1,0:T(8,128)}), f32[64,16,128]{2,1,0:T(8,128)S(1)}, u32[]{:S(2)}, u32[]{:S(2)}) %all-to-all-start.5) | async-done | bytes 524320 | tf_op jit(solution)/shard_map/all_to_all | solution.py:258
  (35 shorter events, 4.8 us)
Async XLA Ops:
  1.3 1.2 copy-start.5
  2.5 0.8 copy-start.9
  3.3 0.8 copy-start.11
  4.2 0.7 copy-start.17
  4.8 0.7 copy-start.20
  49.0 7.6 %copy-start.10 = (bf16[128,256]{1,0:T(8,128)(2,1)S(1)}, bf16[128,256]{1,0:T(8,128)(2,1)}, u32[]{:S(2)}) copy-start(bf16[128,256]{1,0:T(8,128)(2,1)} %w_left.5) | copy-start | bytes 196612
  49.0 7.6 %copy-start.12 = (bf16[128,256]{1,0:T(8,128)(2,1)S(1)}, bf16[128,256]{1,0:T(8,128)(2,1)}, u32[]{:S(2)}) copy-start(bf16[128,256]{1,0:T(8,128)(2,1)} %w_right.5) | copy-start | bytes 196612
  49.0 7.6 %copy-start.14 = (bf16[128,128]{1,0:T(8,128)(2,1)S(1)}, bf16[128,128]{1,0:T(8,128)(2,1)}, u32[]{:S(2)}) copy-start(bf16[128,128]{1,0:T(8,128)(2,1)} %w_gate.3) | copy-start | bytes 98308
  50.4 1.0 copy-start.4
  51.4 23.0 %all-to-all-start.1 = ((bf16[64,64,128]{2,1,0:T(8,128)(2,1)}), bf16[64,64,128]{2,1,0:T(8,128)(2,1)}, u32[]{:S(2)}, u32[]{:S(2)}) async-start(bf16[64,64,128]{2,1,0:T(8,128)(2,1)} %copy-done.4), calls=%async_computation.1 | async-start | bytes 2097152 | tf_op jit(solution)/shard_map/all_to_all | solution.py:258
  56.6 17.9 %copy-start.13 = (bf16[128,128]{1,0:T(8,128)(2,1)S(1)}, bf16[128,128]{1,0:T(8,128)(2,1)}, u32[]{:S(2)}) copy-start(bf16[128,128]{1,0:T(8,128)(2,1)} %w_out.1) | copy-start | bytes 98308
  56.6 17.9 %copy-start.15 = (f32[128]{0:T(128)S(1)}, f32[128]{0:T(128)}, u32[]{:S(2)}) copy-start(f32[128]{0:T(128)} %param.18) | copy-start | bytes 1540
  56.6 17.8 %copy-start.16 = (f32[128]{0:T(128)S(1)}, f32[128]{0:T(128)}, u32[]{:S(2)}) copy-start(f32[128]{0:T(128)} %param.19) | copy-start | bytes 1540
  56.7 1.2 copy-start.19
  63.1 1.4 copy-start
  81.6 1.0 copy-start.7
  147.2 1.3 copy-start.1
  148.6 1.3 copy-start.3
  149.9 22.7 %copy-start.18 = (f32[128]{0:T(128)S(1)}, f32[128]{0:T(128)}, u32[]{:S(2)}) copy-start(f32[128]{0:T(128)} %param.13) | copy-start | bytes 1540
  149.9 22.7 %copy-start.2 = (bf16[256,4096]{1,0:T(8,128)(2,1)S(1)}, bf16[256,4096]{1,0:T(8,128)(2,1)}, u32[]{:S(2)}) copy-start(bf16[256,4096]{1,0:T(8,128)(2,1)} %copy-done.1) | copy-start | bytes 6291460
  168.1 16.9 %all-to-all-start.5 = ((f32[64,16,128]{2,1,0:T(8,128)}), f32[64,16,128]{2,1,0:T(8,128)S(1)}, u32[]{:S(2)}, u32[]{:S(2)}) async-start(f32[64,16,128]{2,1,0:T(8,128)} %shard_map.161), calls=%async_computation.5 | async-start | bytes 1048576 | tf_op jit(solution)/shard_map/all_to_all | solution.py:258
  172.6 1.2 copy-start.6
  173.8 1.2 copy-start.8

commit v2 on v1

v2 whole, which is shorter than its diff:
```python
import functools

import jax
import jax.numpy as jnp
from jax import lax
from jax.experimental import pallas as pl
from jax.experimental.pallas import tpu as pltpu
from jax.sharding import PartitionSpec as P

AXES = ("row", "col")
BF = jnp.bfloat16
F32 = jnp.float32
PAIRS = 16
CHUNK = 8
CELLS = PAIRS * 128
LIMIT = 32 * 1024 * 1024
EPS = 1e-05


def dot(lhs, rhs, left_dim, right_dim):
    return lax.dot_general(
        lhs, rhs, (((left_dim,), (right_dim,)), ((), ())), preferred_element_type=F32
    )


def column(ref):
    return jnp.transpose(jnp.broadcast_to(ref[...], (128, 128)))[:, :1]


def normalize(values):
    centered = values - jnp.mean(values, axis=0, keepdims=True)
    inverse = lax.rsqrt(jnp.mean(centered * centered, axis=0, keepdims=True) + EPS)
    return centered * inverse, inverse


def normalize_backward(grad_hat, normed, inverse):
    return inverse * (
        grad_hat
        - jnp.mean(grad_hat, axis=0, keepdims=True)
        - normed * jnp.mean(grad_hat * normed, axis=0, keepdims=True)
    )


def spans():
    return [(p, p * 128) for p in range(0, PAIRS, CHUNK)]


def load_transposed(ref, first):
    rows = [ref[half, first + p] for p in range(CHUNK) for half in range(2)]
    return jnp.transpose(jnp.concatenate(rows, axis=0)).astype(F32)


def store_transposed(ref, first, values):
    rows = jnp.transpose(values.astype(BF))
    for p in range(CHUNK):
        for half in range(2):
            start = (2 * p + half) * 64
            ref[half, first + p] = rows[start : start + 64]


def lanes(cell):
    return slice(cell, cell + CHUNK * 128)


def low_half(dims):
    return lax.broadcasted_iota(jnp.int32, dims, len(dims) - 1) < 64


def pack(values, first, scr):
    for p in range(CHUNK):
        scr[pl.ds(first + p, 64, stride=PAIRS), :] = values[:, p * 128 : (p + 1) * 128]


def packed(scr):
    return scr[...].reshape(64, PAIRS, 128).astype(BF)


def spread(payload, scr):
    scr[...] = payload.astype(F32).reshape(64 * PAIRS, 128)


def unpack(scr, first):
    return jnp.concatenate(
        [scr[pl.ds(first + p, 64, stride=PAIRS), :] for p in range(CHUNK)], axis=1
    )


def cell_mask(length_ref, first):
    cells = lax.broadcasted_iota(jnp.int32, (1, CHUNK * 128), 1)
    pair = pl.program_id(0) * PAIRS + first + cells // 128
    row = lax.axis_index("row") * 64 + pair + 32 * ((cells // 64) % 2)
    col = lax.axis_index("col") * 64 + cells % 64
    length = length_ref[0]
    return ((row < length) & (col < length)).astype(F32)


def half_weights(ref_left, ref_right, half):
    parts = []
    for ref in (ref_left, ref_right):
        turned = jnp.transpose(ref[...])
        for start in (half * 64, 128 + half * 64):
            parts.append(turned[start : start + 64])
    return jnp.concatenate(parts, axis=0)


def operands_kernel(
    pair, length, gain_ref, bias_ref, w_left, w_right, send, zn_out, *scratch
):
    gain, bias = column(gain_ref), column(bias_ref)
    weights = [half_weights(w_left, w_right, half) for half in range(2)]
    for first, cell in spans():
        zhat, _ = normalize(load_transposed(pair, first))
        zn = (zhat * gain + bias).astype(BF)
        zn_out[:, lanes(cell)] = zn
        mask = cell_mask(length, first)
        for half in range(2):
            both = dot(weights[half], zn, 1, 0)
            for which in range(2):
                value = both[which * 128 : which * 128 + 64]
                sigma = jax.nn.sigmoid(both[which * 128 + 64 : which * 128 + 128])
                pack(mask * sigma * value, first, scratch[2 * half + which])
    for half in range(2):
        for which in range(2):
            send[:, 2 * half + which] = packed(scratch[2 * half + which])


def factors_kernel(
    zn_ref, length, cot, gain_ref, w_left, w_right, w_gate, w_out, sl, gl, sr, gr, hat_grad
):
    gain = column(gain_ref)
    for first, cell in spans():
        here = lanes(cell)
        zn = zn_ref[:, here]
        mask = cell_mask(length, first)
        gate = jax.nn.sigmoid(dot(w_gate[...], zn, 0, 0))
        d_proj = (load_transposed(cot, first) * gate).astype(BF)
        hat_grad[:, here] = dot(w_out[...], d_proj, 1, 0) * gain
        for weights, slope, bend in ((w_left, sl, gl), (w_right, sr, gr)):
            value = dot(weights[...], zn, 0, 0)
            sigma = jax.nn.sigmoid(value[128:])
            slope[:, here] = (mask * sigma).astype(BF)
            bend[:, here] = (mask * value[:128] * sigma * (1.0 - sigma)).astype(BF)


def tile_lanes(col):
    return slice(col * 128, (col + 1) * 128)


def gather_map(got, which, scr):
    for r in range(8):
        for c in range(8):
            scr[r * 32 : (r + 1) * 32, tile_lanes(c)] = got[r * 8 + c, which]


def spread_rows(got, which, scr):
    low = low_half((32, 128))
    for r in range(8):
        for c in range(8):
            tile = got[r * 8 + c, which].astype(F32)
            turned = pltpu.roll(tile, 64, 1)
            blocks = (
                jnp.where(low, tile, 0.0),
                jnp.where(low, turned, 0.0),
                jnp.where(low, 0.0, turned),
                jnp.where(low, 0.0, tile),
            )
            scr[r * 128 : (r + 1) * 128, tile_lanes(c)] = jnp.concatenate(blocks, axis=0).astype(BF)


def product_kernel(got, send, a_scr, b_scr):
    for half in range(2):
        gather_map(got, 2 * half, a_scr)
        spread_rows(got, 2 * half + 1, b_scr)
        for n in range(4):
            out = dot(a_scr[...], b_scr[n * 256 : (n + 1) * 256, :], 1, 1).astype(BF)
            for r in range(8):
                for c in range(2):
                    send[r * 8 + 2 * n + c, half] = out[r * 32 : (r + 1) * 32, tile_lanes(c)]


def middle_kernel(
    got, hat_grad, gain_ref, bias_ref, send, y_out, scr_0, scr_1, out_0, out_1
):
    spread(got[:, 0], scr_0)
    spread(got[:, 1], scr_1)
    gain, bias = column(gain_ref), column(bias_ref)
    for first, cell in spans():
        here = lanes(cell)
        values = jnp.concatenate([unpack(scr_0, first), unpack(scr_1, first)], axis=0)
        hat, inverse = normalize(values)
        d_prod = normalize_backward(hat_grad[:, here], hat, inverse)
        pack(d_prod[:64], first, out_0)
        pack(d_prod[64:], first, out_1)
        y_out[:, here] = (hat * gain + bias).astype(BF)
    send[:, 0] = packed(out_0)
    send[:, 1] = packed(out_1)


def updated_kernel(y_ref, zn_ref, cot, w_out, w_gate, updated, dg_out, grad_out, grad_gate):
    @pl.when(pl.program_id(0) == 0)
    def _():
        grad_out[...] = jnp.zeros((128, 128), F32)
        grad_gate[...] = jnp.zeros((128, 128), F32)

    for first, cell in spans():
        here = lanes(cell)
        y, zn = y_ref[:, here], zn_ref[:, here]
        gate = jax.nn.sigmoid(dot(w_gate[...], zn, 0, 0))
        upstream = load_transposed(cot, first)
        proj = dot(w_out[...], y, 0, 0)
        d_proj = (upstream * gate).astype(BF)
        d_gpre = (upstream * proj * gate * (1.0 - gate)).astype(BF)
        store_transposed(updated, first, gate * proj)
        dg_out[:, here] = d_gpre
        grad_out[...] += dot(y, d_proj, 1, 1)
        grad_gate[...] += dot(zn, d_gpre, 1, 1)


def product_grads_kernel(got, operands_ref, send, a_scr, b_scr, d_scr):
    low = low_half((32, 128))
    for half in range(2):
        gather_map(operands_ref, 2 * half, a_scr)
        spread_rows(operands_ref, 2 * half + 1, b_scr)
        gather_map(got, half, d_scr)
        for n in range(4):
            out = dot(d_scr[...], b_scr[:, n * 256 : (n + 1) * 256], 1, 0).astype(BF)
            for r in range(8):
                for c in range(2):
                    send[r * 8 + 2 * n + c, 2 * half] = out[r * 32 : (r + 1) * 32, tile_lanes(c)]
        for m in range(2):
            out = dot(d_scr[:, m * 512 : (m + 1) * 512], a_scr[...], 0, 0)
            for r in range(4):
                for c in range(8):
                    block = out[r * 128 : (r + 1) * 128, tile_lanes(c)]
                    same = jnp.where(low, block[:32], block[96:])
                    cross = jnp.where(low, block[32:64], block[64:96])
                    send[(m * 4 + r) * 8 + c, 2 * half + 1] = (
                        same + pltpu.roll(cross, 64, 1)
                    ).astype(BF)


def weights_kernel(
    got, zn, sl, gl, sr, gr, grad_gate, grad_out, dl_out, dr_out, send, acc, stage, scr_0, scr_1
):
    @pl.when(pl.program_id(0) == 0)
    def _():
        acc[...] = jnp.zeros((128, 512), F32)

    for which, slope, bend, out in ((0, sl, gl, dl_out), (1, sr, gr, dr_out)):
        spread(got[:, which], scr_0)
        spread(got[:, 2 + which], scr_1)
        for first, cell in spans():
            here = lanes(cell)
            grad = jnp.concatenate([unpack(scr_0, first), unpack(scr_1, first)], axis=0)
            value = jnp.concatenate(
                [grad * slope[:, here], grad * bend[:, here]], axis=0
            ).astype(BF)
            out[:, here] = value
            acc[:, which * 256 : (which + 1) * 256] += dot(zn[:, here], value, 1, 1)

    @pl.when(pl.program_id(0) == pl.num_programs(0) - 1)
    def _():
        for t in range(6):
            if t < 4:
                tile = acc[:, tile_lanes(t)]
            else:
                tile = (grad_gate if t == 4 else grad_out)[...]
            for half in range(2):
                stage[pl.ds(2 * t + half, 64, stride=16), :] = tile[half * 64 : (half + 1) * 64]
        for t in range(12, 16):
            stage[pl.ds(t, 64, stride=16), :] = jnp.zeros((64, 128), F32)
        send[...] = stage[...].reshape(64, 16, 128).astype(BF)


def pair_kernel(pair, gain_ref, dl, dr, dg, w_left, w_right, w_gate, out):
    gain = column(gain_ref)
    for first, cell in spans():
        here = lanes(cell)
        zhat, inverse = normalize(load_transposed(pair, first))
        d_zn = (
            dot(w_left[...], dl[:, here], 1, 0)
            + dot(w_right[...], dr[:, here], 1, 0)
            + dot(w_gate[...], dg[:, here], 1, 0)
        )
        store_transposed(out, first, normalize_backward(d_zn * gain, zhat, inverse))


def sum_kernel(scale, got, send):
    total = got[0].astype(F32)
    for s in range(1, 64):
        total = total + got[s].astype(F32)
    send[...] = jnp.broadcast_to((total * scale).astype(BF)[None], send.shape)


def split_kernel(got, left, right, gate, out, stage):
    stage[...] = got[...].astype(F32).reshape(1024, 128)
    for t, (ref, lane) in enumerate(
        ((left, 0), (left, 128), (right, 0), (right, 128), (gate, 0), (out, 0))
    ):
        for half in range(2):
            ref[half * 64 : (half + 1) * 64, lane : lane + 128] = stage[
                pl.ds(2 * t + half, 64, stride=16), :
            ]


def call(kernel, grid, in_specs, out_specs, out_shape, scratch=(), cost=(10**9, 10**7)):
    return pl.pallas_call(
        kernel,
        grid=grid,
        in_specs=in_specs,
        out_specs=out_specs,
        out_shape=out_shape,
        scratch_shapes=list(scratch),
        cost_estimate=pl.CostEstimate(flops=cost[0], bytes_accessed=cost[1], transcendentals=0),
        compiler_params=pltpu.CompilerParams(vmem_limit_bytes=LIMIT),
    )


def whole(*dims):
    return pl.BlockSpec(dims, lambda *_: (0,) * len(dims))


def shape(dims, kind, space=None):
    return jax.ShapeDtypeStruct(dims, kind) if space is None else space(dims, kind)


def keep(value, space):
    return pltpu.with_memory_space_constraint(value, space)


def exchange(values):
    owners = values.shape[0]
    flat = values.reshape(owners, -1, 128)
    return lax.all_to_all(flat, AXES, 0, 0, tiled=True).reshape(values.shape)


def body(
    pair, length, ln_in_gain, ln_in_bias, w_left, w_right, w_gate,
    product_norm_gain, product_norm_bias, w_out, cotangent,
):
    tile_i, tile_j, chans = pair.shape
    total = tile_j * lax.axis_size("col")
    cells = tile_i * tile_j
    grid = (32 // PAIRS,)
    gain_in, bias_in = ln_in_gain.reshape(1, 128), ln_in_bias.reshape(1, 128)
    gain_p, bias_p = product_norm_gain.reshape(1, 128), product_norm_bias.reshape(1, 128)
    halves = (2, tile_i // 2, tile_j, chans)
    pair = keep(pair.reshape(halves), pltpu.HBM)
    cotangent = keep(cotangent.reshape(halves), pltpu.HBM)
    w_left, w_right, w_gate, w_out = (
        keep(w, pltpu.HBM) for w in (w_left, w_right, w_gate, w_out)
    )

    natural = pl.BlockSpec((2, PAIRS, 64, 128), lambda i: (0, i, 0, 0))
    chan_major = pl.BlockSpec((128, CELLS), lambda i: (0, i))
    chan_major2 = pl.BlockSpec((256, CELLS), lambda i: (0, i))
    double = pl.BlockSpec((64, 2, PAIRS, 128), lambda i: (0, 0, i, 0))
    quad = pl.BlockSpec((64, 4, PAIRS, 128), lambda i: (0, 0, i, 0))
    scalar = pl.BlockSpec(memory_space=pltpu.SMEM)
    vec, wide, square = whole(1, 128), whole(128, 256), whole(128, 128)
    swap = pltpu.VMEM((64 * PAIRS, 128), F32)
    near, far = pltpu.VMEM, pltpu.HBM
    b_cells = shape((128, cells), BF, far)
    pay2, pay4 = shape((64, 2, 32, 128), BF, far), shape((64, 4, 32, 128), BF, far)
    f_square = shape((128, 128), F32, far)
    a_map, b_map = pltpu.VMEM((256, 1024), BF), pltpu.VMEM((1024, 1024), BF)

    send, zn = call(
        operands_kernel, grid,
        [natural, scalar, vec, vec, wide, wide],
        [quad, chan_major],
        [pay4, b_cells],
        [swap] * 4,
    )(pair, length, gain_in, bias_in, w_left, w_right)
    zn = keep(zn, far)
    operands = exchange(send)

    *factors, hat_grad = call(
        factors_kernel, grid,
        [chan_major, scalar, natural, vec, wide, wide, square, square],
        [chan_major] * 5,
        [b_cells] * 4 + [shape((128, cells), F32, far)],
    )(zn, length, cotangent, gain_p, w_left, w_right, w_gate, w_out)
    factors = [keep(f, far) for f in factors]

    product = call(
        product_kernel, (1,), [whole(64, 4, 32, 128)], whole(64, 2, 32, 128), pay2, [a_map, b_map]
    )(keep(operands, near))

    send, y = call(
        middle_kernel, grid,
        [double, chan_major, vec, vec],
        [double, chan_major],
        [pay2, b_cells],
        [swap] * 4,
    )(keep(exchange(product), near), keep(hat_grad, far), gain_p, bias_p)
    got = exchange(send)

    updated, d_gpre, grad_out, grad_gate = call(
        updated_kernel, grid,
        [chan_major, chan_major, natural, square, square],
        [natural, chan_major, square, square],
        [shape(halves, BF, far), b_cells, f_square, f_square],
    )(keep(y, far), zn, cotangent, w_out, w_gate)

    send = call(
        product_grads_kernel, (1,),
        [whole(64, 2, 32, 128), whole(64, 4, 32, 128)],
        whole(64, 4, 32, 128),
        pay4,
        [a_map, b_map, a_map],
    )(keep(got, near), keep(operands, near))

    d_left, d_right, terms = call(
        weights_kernel, grid,
        [quad] + [chan_major] * 5 + [square, square],
        [chan_major2, chan_major2, whole(64, 16, 128)],
        [shape((256, cells), BF, far)] * 2 + [shape((64, 16, 128), BF, far)],
        [pltpu.VMEM((128, 512), F32), pltpu.VMEM((1024, 128), F32), swap, swap],
    )(keep(exchange(send), near), zn, *factors, keep(grad_gate, far), keep(grad_out, far))
    shares = exchange(terms)

    d_pair = call(
        pair_kernel, grid,
        [natural, vec, chan_major2, chan_major2, chan_major, wide, wide, square],
        natural,
        shape(halves, BF, far),
    )(pair, gain_in, keep(d_left, far), keep(d_right, far), keep(d_gpre, far), w_left, w_right, w_gate)

    summed = call(
        functools.partial(sum_kernel, 1.0 / total), (1,),
        [whole(64, 16, 128)], whole(64, 16, 128), shape((64, 16, 128), BF, far), cost=(10**6, 10**6),
    )(shares)
    sums = call(
        split_kernel, (1,),
        [whole(64, 16, 128)],
        [wide, wide, square, square],
        [shape((128, 256), F32)] * 2 + [shape((128, 128), F32)] * 2,
        [pltpu.VMEM((1024, 128), F32)],
        cost=(10**6, 10**6),
    )(exchange(summed))
    full = (tile_i, tile_j, chans)
    return (updated.reshape(full), d_pair.reshape(full), *sums)


def solution(mesh):
    in_specs = (
        P(("rep", "row"), "col", None),
        P("rep"),
        P(),
        P(),
        P(),
        P(),
        P(),
        P(),
        P(),
        P(),
        P(("rep", "row"), "col", None),
    )
    out_specs = (
        P(("rep", "row"), "col", None),
        P(("rep", "row"), "col", None),
        P("rep", None),
        P("rep", None),
        P("rep", None),
        P("rep", None),
    )
    return jax.shard_map(body, mesh=mesh, in_specs=in_specs, out_specs=out_specs, check_vma=False)
```

time: 187 us -> 176 us (0.941)
  blocking collectives: 112 us -> 76.5 us
  waiting for transfers between devices: 15.1 us -> 40.7 us
  local copies, waits for them, and re-layouts: 13.9 us -> 1.32 us
  Pallas kernels: 34.2 us -> 41.7 us
  starting transfers between devices: 9.64 us -> 13.9 us
    all_to_all x4 -> x3, blocking collectives: 112 us -> 76.5 us  [exchange(): return lax.all_to_all(flat, AXES, 0, 0, tiled=True).reshape(values.shape)]
    all_to_all x2 -> x3, waiting for transfers between devices: 15.1 us -> 40.7 us  [exchange(): return lax.all_to_all(flat, AXES, 0, 0, tiled=True).reshape(values.shape)]
    unnamed x42 -> x10, local copies, waits for them, and re-layouts: 13.9 us -> 1.32 us
    pallas_call x7 -> x8, Pallas kernels: 28.5 us -> 36.1 us  [the longest x1 6.92 us: body(): call(weights_kernel, grid, [quad] + [chan_major] * 5 + [square, square],...]
    all_to_all x2 -> x3, starting transfers between devices: 9.64 us -> 13.9 us  [exchange(): return lax.all_to_all(flat, AXES, 0, 0, tiled=True).reshape(values.shape)]
  transfers between devices with their start and end apart: 2 -> 3, of which waited for: 2 -> 3; matrix products, arithmetic and copies ran while one was open for 0% -> 0% of each run, Pallas kernels for 5% -> 9%
where the time goes in v2:
time: 176 us; the launch traced here: 175 us
  blocking collectives  76.5 us (43%)
  Pallas kernels  41.7 us (24%)
  waiting for transfers between devices  40.7 us (23%)
  starting transfers between devices  13.9 us (8%)
    all_to_all x3, blocking collectives, exchange(): return lax.all_to_all(flat, AXES, 0, 0, tiled=True).reshape(values.shape)  76.5 us
    all_to_all x3, waiting for transfers between devices, exchange(): return lax.all_to_all(flat, AXES, 0, 0, tiled=True).reshape(values.shape)  40.7 us
    all_to_all x3, starting transfers between devices, exchange(): return lax.all_to_all(flat, AXES, 0, 0, tiled=True).reshape(values.shape)  13.9 us
    pallas_call x1, Pallas kernels, body(): call(weights_kernel, grid, [quad] + [chan_major] * 5 + [square, square],...  6.92 us
    pallas_call x1, Pallas kernels, body(): call(factors_kernel, grid, [chan_major, scalar, natural, vec, wide, wide,...  5.75 us
    pallas_call x1, Pallas kernels, body(): call(middle_kernel, grid, [double, chan_major, vec, vec], [double, chan_m...  5.47 us
    pallas_call x1, Pallas kernels, body(): call(operands_kernel, grid, [natural, scalar, vec, vec, wide, wide], [qua...  5.22 us
    pallas_call x1, Pallas kernels, body(): call(pair_kernel, grid, [natural, vec, chan_major2, chan_major2, chan_maj...  4.84 us
  transfers between devices with their start and end apart: 3, of which 3 were waited for; matrix products, arithmetic and copies ran while one was open for 0% of the time, Pallas kernels for 9%

profile of v2, /device:TPU:1, one launch (start us, length us, event | category | flops | bytes accessed | tf_op | source)
XLA Modules:
  0.0 175.5 jit_solution(7154230906248372813)
XLA Ops:
  1.3 0.0 copy-start
  1.3 0.6 copy-done
  1.9 0.7 copy-done.2
  2.6 5.2 %shard_map.154 = (bf16[64,4,32,128]{3,2,1,0:T(8,128)(2,1)}, bf16[128,4096]{1,0:T(8,128)(2,1)}) custom-call(bf16[2,32,64,128]{3,2,1,0:T(8,128)(2,1)} %bitcast.31, s32[1]{0:T(128)S(6)} %copy.17.length, f32[1,128]{1,0:T(1,128)S(1)} %bitcast.21, f32[1,128]{1,0:T(1,128)S(1)} %bitcast.23, bf16[128,256]{1,0:T(8,128)(2,1)} %w_left.5, bf16[128,256]{1,0:T(8,128)(2,1)} %w_right.5), custom_call_target="tpu_custom_call" | custom-call | flops 1000000000 | bytes 10000000 | tf_op jit(solution)/shard_map/pallas_call | solution.py:368
  7.8 39.4 %all_to_all.30 = bf16[64,128,128]{2,1,0:T(8,128)(2,1)S(1)} all-to-all(bf16[64,128,128]{2,1,0:T(8,128)(2,1)} %bitcast.28), channel_id=1, replica_groups=mesh['row'=8,'col'=8,'rep'=2] {'row','col'}, dimensions={0} | all-to-all | bytes 4194304 | tf_op jit(solution)/shard_map/all_to_all | solution.py:334
  47.2 2.7 %shard_map.155 = bf16[64,2,32,128]{3,2,1,0:T(8,128)(2,1)} custom-call(bf16[64,4,32,128]{3,2,1,0:T(8,128)(2,1)S(1)} %bitcast.17), custom_call_target="tpu_custom_call" | custom-call | flops 1000000000 | bytes 10000000 | tf_op jit(solution)/shard_map/pallas_call | solution.py:386
  49.9 5.0 %all-to-all-start.1 = ((bf16[64,64,128]{2,1,0:T(8,128)(2,1)}), bf16[64,64,128]{2,1,0:T(8,128)(2,1)S(1)}, u32[]{:S(2)}, u32[]{:S(2)}) async-start(bf16[64,64,128]{2,1,0:T(8,128)(2,1)} %bitcast.29), calls=%async_computation.1 | async-start | bytes 2097152 | tf_op jit(solution)/shard_map/all_to_all | solution.py:334
  54.9 0.0 copy-start.4
  54.9 0.0 copy-done.3
  54.9 5.7 %shard_map.156 = (bf16[128,4096]{1,0:T(8,128)(2,1)}, bf16[128,4096]{1,0:T(8,128)(2,1)}, bf16[128,4096]{1,0:T(8,128)(2,1)}, bf16[128,4096]{1,0:T(8,128)(2,1)}, f32[128,4096]{1,0:T(8,128)}) custom-call(bf16[128,4096]{1,0:T(8,128)(2,1)} %get-tuple-element.27.zn_ref.zn, s32[1]{0:T(128)S(6)} %copy.17.length, bf16[2,32,64,128]{3,2,1,0:T(8,128)(2,1)} %bitcast.34, ...), custom_call_target="tpu_custom_call" | custom-call | flops 1000000000 | bytes 10000000 | tf_op jit(solution)/shard_map/pallas_call | solution.py:378
  60.7 12.2 %all-to-all-done.1 = bf16[64,64,128]{2,1,0:T(8,128)(2,1)S(1)} async-done(((bf16[64,64,128]{2,1,0:T(8,128)(2,1)}), bf16[64,64,128]{2,1,0:T(8,128)(2,1)S(1)}, u32[]{:S(2)}, u32[]{:S(2)}) %all-to-all-start.1) | async-done | bytes 1048608 | tf_op jit(solution)/shard_map/all_to_all | solution.py:334
  72.9 5.5 %shard_map.157 = (bf16[64,2,32,128]{3,2,1,0:T(8,128)(2,1)}, bf16[128,4096]{1,0:T(8,128)(2,1)}) custom-call(bf16[64,2,32,128]{3,2,1,0:T(8,128)(2,1)S(1)} %bitcast.20, f32[128,4096]{1,0:T(8,128)} %get-tuple-element.28.hat_grad, f32[1,128]{1,0:T(1,128)S(1)} %bitcast.25, f32[1,128]{1,0:T(1,128)S(1)} %bitcast.26), custom_call_target="tpu_custom_call" | custom-call | flops 1000000000 | bytes 10000000 | tf_op jit(solution)/shard_map/pallas_call | solution.py:390
  78.3 22.4 %all_to_all.31 = bf16[64,64,128]{2,1,0:T(8,128)(2,1)S(1)} all-to-all(bf16[64,64,128]{2,1,0:T(8,128)(2,1)} %bitcast.30), channel_id=1, replica_groups=mesh['row'=8,'col'=8,'rep'=2] {'row','col'}, dimensions={0} | all-to-all | bytes 2097152 | tf_op jit(solution)/shard_map/all_to_all | solution.py:334
  100.7 4.4 %shard_map.159 = bf16[64,4,32,128]{3,2,1,0:T(8,128)(2,1)} custom-call(bf16[64,2,32,128]{3,2,1,0:T(8,128)(2,1)S(1)} %bitcast.19, bf16[64,4,32,128]{3,2,1,0:T(8,128)(2,1)S(1)} %bitcast.18), custom_call_target="tpu_custom_call" | custom-call | flops 1000000000 | bytes 10000000 | tf_op jit(solution)/shard_map/pallas_call | solution.py:406
  105.1 4.4 %all-to-all-start.3 = ((bf16[64,128,128]{2,1,0:T(8,128)(2,1)}), bf16[64,128,128]{2,1,0:T(8,128)(2,1)S(1)}, u32[]{:S(2)}, u32[]{:S(2)}) async-start(bf16[64,128,128]{2,1,0:T(8,128)(2,1)} %bitcast.27), calls=%async_computation.3 | async-start | bytes 4194304 | tf_op jit(solution)/shard_map/all_to_all | solution.py:334
  109.6 4.8 %shard_map.158 = (bf16[2,32,64,128]{3,2,1,0:T(8,128)(2,1)}, bf16[128,4096]{1,0:T(8,128)(2,1)}, f32[128,128]{1,0:T(8,128)}, f32[128,128]{1,0:T(8,128)}) custom-call(bf16[128,4096]{1,0:T(8,128)(2,1)} %get-tuple-element.29.y_ref, bf16[128,4096]{1,0:T(8,128)(2,1)} %get-tuple-element.27.zn_ref.zn, bf16[2,32,64,128]{3,2,1,0:T(8,128)(2,1)} %bitcast.35, ...), custom_call_target="tpu_custom_call" | custom-call | flops 1000000000 | bytes 10000000 | tf_op jit(solution)/shard_map/pallas_call | solution.py:399
  114.4 23.7 %all-to-all-done.3 = bf16[64,128,128]{2,1,0:T(8,128)(2,1)S(1)} async-done(((bf16[64,128,128]{2,1,0:T(8,128)(2,1)}), bf16[64,128,128]{2,1,0:T(8,128)(2,1)S(1)}, u32[]{:S(2)}, u32[]{:S(2)}) %all-to-all-start.3) | async-done | bytes 2097184 | tf_op jit(solution)/shard_map/all_to_all | solution.py:334
  138.1 6.9 %shard_map.160 = (bf16[256,4096]{1,0:T(8,128)(2,1)}, bf16[256,4096]{1,0:T(8,128)(2,1)}, bf16[64,16,128]{2,1,0:T(8,128)(2,1)}) custom-call(bf16[64,4,32,128]{3,2,1,0:T(8,128)(2,1)S(1)} %bitcast.16, bf16[128,4096]{1,0:T(8,128)(2,1)} %get-tuple-element.27.zn_ref.zn, bf16[128,4096]{1,0:T(8,128)(2,1)} %get-tuple-element.32.sl, ...), custom_call_target="tpu_custom_call" | custom-call | flops 1000000000 | bytes 10000000 | tf_op jit(solution)/shard_map/pallas_call | solution.py:414
  145.0 14.7 %all_to_all.32.got = bf16[64,16,128]{2,1,0:T(8,128)(2,1)S(1)} all-to-all(bf16[64,16,128]{2,1,0:T(8,128)(2,1)} %get-tuple-element.41), channel_id=1, replica_groups=mesh['row'=8,'col'=8,'rep'=2] {'row','col'}, dimensions={0} | all-to-all | bytes 524288 | tf_op jit(solution)/shard_map/all_to_all | solution.py:334
  159.7 0.8 shard_map.162
  160.5 4.5 %all-to-all-start.5 = ((bf16[64,16,128]{2,1,0:T(8,128)(2,1)}), bf16[64,16,128]{2,1,0:T(8,128)(2,1)S(1)}, u32[]{:S(2)}, u32[]{:S(2)}) async-start(bf16[64,16,128]{2,1,0:T(8,128)(2,1)} %shard_map.162), calls=%async_computation.5 | async-start | bytes 524288 | tf_op jit(solution)/shard_map/all_to_all | solution.py:334
  165.0 4.8 %shard_map.161 = bf16[2,32,64,128]{3,2,1,0:T(8,128)(2,1)} custom-call(bf16[2,32,64,128]{3,2,1,0:T(8,128)(2,1)} %bitcast.32, f32[1,128]{1,0:T(1,128)S(1)} %bitcast.22, bf16[256,4096]{1,0:T(8,128)(2,1)} %get-tuple-element.38.dl, bf16[256,4096]{1,0:T(8,128)(2,1)} %get-tuple-element.39.dr, bf16[128,4096]{1,0:T(8,128)(2,1)} %get-tuple-element.40.dg, ...), custom_call_target="tpu_custom_call" | custom-call | flops 1000000000 | bytes 10000000 | tf_op jit(solution)/shard_map/pallas_call | solution.py:423
  169.8 4.8 %all-to-all-done.5.got = bf16[64,16,128]{2,1,0:T(8,128)(2,1)S(1)} async-done(((bf16[64,16,128]{2,1,0:T(8,128)(2,1)}), bf16[64,16,128]{2,1,0:T(8,128)(2,1)S(1)}, u32[]{:S(2)}, u32[]{:S(2)}) %all-to-all-start.5) | async-done | bytes 262176 | tf_op jit(solution)/shard_map/all_to_all | solution.py:334
  174.7 0.8 shard_map.163
  (5 shorter events, 0.0 us)
Async XLA Ops:
  1.3 0.7 copy-start
  1.9 0.7 copy-start.2
  47.2 7.7 %copy-start.3 = (f32[128]{0:T(128)S(1)}, f32[128]{0:T(128)}, u32[]{:S(2)}) copy-start(f32[128]{0:T(128)} %param.18) | copy-start | bytes 1540
  49.9 22.9 %all-to-all-start.1 = ((bf16[64,64,128]{2,1,0:T(8,128)(2,1)}), bf16[64,64,128]{2,1,0:T(8,128)(2,1)S(1)}, u32[]{:S(2)}, u32[]{:S(2)}) async-start(bf16[64,64,128]{2,1,0:T(8,128)(2,1)} %bitcast.29), calls=%async_computation.1 | async-start | bytes 2097152 | tf_op jit(solution)/shard_map/all_to_all | solution.py:334
  54.9 17.9 %copy-start.4 = (f32[128]{0:T(128)S(1)}, f32[128]{0:T(128)}, u32[]{:S(2)}) copy-start(f32[128]{0:T(128)} %param.19) | copy-start | bytes 1540
  105.1 32.9 %all-to-all-start.3 = ((bf16[64,128,128]{2,1,0:T(8,128)(2,1)}), bf16[64,128,128]{2,1,0:T(8,128)(2,1)S(1)}, u32[]{:S(2)}, u32[]{:S(2)}) async-start(bf16[64,128,128]{2,1,0:T(8,128)(2,1)} %bitcast.27), calls=%async_computation.3 | async-start | bytes 4194304 | tf_op jit(solution)/shard_map/all_to_all | solution.py:334
  138.1 26.9 %copy-start.1 = (f32[128]{0:T(128)S(1)}, f32[128]{0:T(128)}, u32[]{:S(2)}) copy-start(f32[128]{0:T(128)} %param.13) | copy-start | bytes 1540
  160.5 14.2 %all-to-all-start.5 = ((bf16[64,16,128]{2,1,0:T(8,128)(2,1)}), bf16[64,16,128]{2,1,0:T(8,128)(2,1)S(1)}, u32[]{:S(2)}, u32[]{:S(2)}) async-start(bf16[64,16,128]{2,1,0:T(8,128)(2,1)} %shard_map.162), calls=%async_computation.5 | async-start | bytes 524288 | tf_op jit(solution)/shard_map/all_to_all | solution.py:334

commit v3 on v2

v3 whole, which is shorter than its diff:
```python
import functools

import jax
import jax.numpy as jnp
from jax import lax
from jax.experimental import pallas as pl
from jax.experimental.pallas import tpu as pltpu
from jax.sharding import PartitionSpec as P

AXES = ("row", "col")
BF = jnp.bfloat16
F32 = jnp.float32
STEP = 16
ROWS = 16
PITCH = 17
CELLS = STEP * 64
LIMIT = 32 * 1024 * 1024
EPS = 1e-05


def dot(lhs, rhs, left_dim, right_dim):
    return lax.dot_general(
        lhs, rhs, (((left_dim,), (right_dim,)), ((), ())), preferred_element_type=F32
    )


def column(ref):
    return jnp.transpose(jnp.broadcast_to(ref[...], (128, 128)))[:, :1]


def normalize(values):
    centered = values - jnp.mean(values, axis=0, keepdims=True)
    inverse = lax.rsqrt(jnp.mean(centered * centered, axis=0, keepdims=True) + EPS)
    return centered * inverse, inverse


def normalize_backward(grad_hat, normed, inverse):
    return inverse * (
        grad_hat
        - jnp.mean(grad_hat, axis=0, keepdims=True)
        - normed * jnp.mean(grad_hat * normed, axis=0, keepdims=True)
    )


def sigmoid(values):
    return 0.5 * jnp.tanh(0.5 * values) + 0.5


def spans(rows):
    return [(i, slice(i * 64, (i + rows) * 64)) for i in range(0, STEP, rows)]


def load_transposed(ref, first, rows):
    return jnp.transpose(ref[first : first + rows].reshape(rows * 64, 128)).astype(F32)


def store_transposed(ref, first, values):
    rows = values.shape[1] // 64
    ref[first : first + rows] = jnp.transpose(values.astype(BF)).reshape(rows, 64, 128)


def low_half(dims):
    return lax.broadcasted_iota(jnp.int32, dims, len(dims) - 1) < 64


def pack(values, first, scr):
    low = low_half((64, 128))
    for t in range(values.shape[1] // 128):
        lane = slice(t * 128, (t + 1) * 128)
        upper, lower = values[:64, lane], values[64:, lane]
        row = first + 2 * t
        scr[pl.ds(row, 64, stride=PITCH), :] = jnp.where(low, upper, pltpu.roll(lower, 64, 1))
        scr[pl.ds(row + 1, 64, stride=PITCH), :] = jnp.where(low, pltpu.roll(upper, 64, 1), lower)


def packed(scr, kind=BF):
    return jnp.stack([scr[d * PITCH : d * PITCH + STEP] for d in range(64)]).astype(kind)


def spread(payload, scr):
    wide = payload.astype(F32)
    for d in range(64):
        scr[d * PITCH : d * PITCH + STEP] = wide[d]


def unpack(scr, first, rows):
    low = low_half((64, 128))
    tiles = []
    for row in range(first, first + rows, 2):
        even = scr[pl.ds(row, 64, stride=PITCH), :]
        odd = scr[pl.ds(row + 1, 64, stride=PITCH), :]
        upper = jnp.where(low, even, pltpu.roll(odd, 64, 1))
        lower = jnp.where(low, pltpu.roll(even, 64, 1), odd)
        tiles.append(jnp.concatenate([upper, lower], axis=0))
    return jnp.concatenate(tiles, axis=1) if len(tiles) > 1 else tiles[0]


def cell_mask(length_ref, first, rows):
    cells = lax.broadcasted_iota(jnp.int32, (1, rows * 64), 1)
    row = lax.axis_index("row") * 64 + pl.program_id(0) * STEP + first + cells // 64
    col = lax.axis_index("col") * 64 + cells % 64
    length = length_ref[0]
    return ((row < length) & (col < length)).astype(F32)


def operands_kernel(pair, length, gain_ref, bias_ref, w_left, w_right, send, zn_out, scr_a, scr_b):
    gain, bias = column(gain_ref), column(bias_ref)
    weights = [jnp.transpose(ref[...]) for ref in (w_left, w_right)]
    for first, here in spans(ROWS):
        zhat, _ = normalize(load_transposed(pair, first, ROWS))
        zn = (zhat * gain + bias).astype(BF)
        zn_out[:, here] = zn
        mask = cell_mask(length, first, ROWS)
        for weight, scr in zip(weights, (scr_a, scr_b)):
            both = dot(weight, zn, 1, 0)
            pack(mask * sigmoid(both[128:]) * both[:128], first, scr)
    rows = pl.ds(pl.multiple_of(pl.program_id(0) * STEP, STEP), STEP)
    send[:, 0, rows] = packed(scr_a)
    send[:, 1, rows] = packed(scr_b)


def factors_kernel(
    zn_ref, length, cot, gain_ref, w_left, w_right, w_gate, w_out,
    sl, gl, sr, gr, hat_grad, zn_cells, scr,
):
    gain = column(gain_ref)
    for first, here in spans(ROWS):
        zn = zn_ref[:, here]
        zn_cells[here] = jnp.transpose(zn)
        mask = cell_mask(length, first, ROWS)
        gate = sigmoid(dot(w_gate[...], zn, 0, 0))
        d_proj = (load_transposed(cot, first, ROWS) * gate).astype(BF)
        pack(dot(w_out[...], d_proj, 1, 0) * gain, first, scr)
        for weights, slope, bend in ((w_left, sl, gl), (w_right, sr, gr)):
            value = dot(weights[...], zn, 0, 0)
            sigma = sigmoid(value[128:])
            slope[:, here] = (mask * sigma).astype(BF)
            bend[:, here] = (mask * value[:128] * sigma * (1.0 - sigma)).astype(BF)
    hat_grad[...] = packed(scr, F32)


def gather_map(got, which, scr):
    for r in range(8):
        for c in range(8):
            scr[r * 64 : (r + 1) * 64, c * 128 : (c + 1) * 128] = got[r * 8 + c, which]


def double_rows(got, which, scr):
    low = low_half((64, 128))
    zero = jnp.zeros((64, 128), BF)
    for r in range(8):
        for c in range(8):
            tile = got[r * 8 + c, which]
            lanes = slice(c * 128, (c + 1) * 128)
            scr[r * 128 : r * 128 + 64, lanes] = jnp.where(low, tile, zero)
            scr[r * 128 + 64 : (r + 1) * 128, lanes] = jnp.where(low, zero, tile)


def product_kernel(got, send, a_scr, b_scr, out_scr, sems):
    gather_map(got, 0, a_scr)
    double_rows(got, 1, b_scr)
    copies = []
    for n in range(4):
        out = dot(a_scr[...], b_scr[n * 256 : (n + 1) * 256, :], 1, 1).astype(BF)
        for r in range(8):
            for c in range(2):
                out_scr[r, 2 * n + c] = out[r * 64 : (r + 1) * 64, c * 128 : (c + 1) * 128]
        part = (slice(None), pl.ds(2 * n, 2))
        copies.append(pltpu.make_async_copy(out_scr.at[part], send.at[part], sems.at[n]))
        copies[-1].start()
    for copy in copies:
        copy.wait()


def halves_sum(values):
    return values + pltpu.roll(values, 64, 1)


def middle_kernel(got, hat_grad, send):
    rows = pl.ds(pl.multiple_of(pl.program_id(0) * STEP, STEP), STEP)

    def value(d):
        return got[d, rows].astype(F32)

    def channel_mean(term):
        sums = [term(d) for d in range(4)]
        for d in range(4, 64):
            sums[d % 4] = sums[d % 4] + term(d)
        return halves_sum((sums[0] + sums[1]) + (sums[2] + sums[3])) * (1.0 / 128)

    mean = channel_mean(value)
    inverse = lax.rsqrt(channel_mean(lambda d: (value(d) - mean) * (value(d) - mean)) + EPS)
    first = channel_mean(lambda d: hat_grad[d])
    second = channel_mean(lambda d: hat_grad[d] * ((value(d) - mean) * inverse))
    for d in range(64):
        hat = (value(d) - mean) * inverse
        send[d, rows] = (inverse * (hat_grad[d] - first - hat * second)).astype(BF)


def updated_kernel(
    product, zn_ref, cot, gain_ref, bias_ref, w_out, w_gate,
    updated, dg_out, grad_out, grad_gate, scr,
):
    @pl.when(pl.program_id(0) == 0)
    def _():
        grad_out[...] = jnp.zeros((128, 128), F32)
        grad_gate[...] = jnp.zeros((128, 128), F32)

    spread(product[...], scr)
    gain, bias = column(gain_ref), column(bias_ref)
    for first, here in spans(ROWS):
        hat, _ = normalize(unpack(scr, first, ROWS))
        y = (hat * gain + bias).astype(BF)
        zn = zn_ref[:, here]
        gate = sigmoid(dot(w_gate[...], zn, 0, 0))
        upstream = load_transposed(cot, first, ROWS)
        proj = dot(w_out[...], y, 0, 0)
        d_proj = (upstream * gate).astype(BF)
        d_gpre = (upstream * proj * gate * (1.0 - gate)).astype(BF)
        store_transposed(updated, first, gate * proj)
        dg_out[:, here] = d_gpre
        grad_out[...] += dot(y, d_proj, 1, 1)
        grad_gate[...] += dot(zn, d_gpre, 1, 1)


def product_grads_kernel(got, operands_ref, send, a_scr, b_scr, d_scr):
    gather_map(operands_ref, 0, a_scr)
    double_rows(operands_ref, 1, b_scr)
    for r in range(8):
        for c in range(8):
            d_scr[r * 64 : (r + 1) * 64, c * 128 : (c + 1) * 128] = got[r * 8 + c]
    for n in range(4):
        out = dot(d_scr[...], b_scr[:, n * 256 : (n + 1) * 256], 1, 0).astype(BF)
        for r in range(8):
            for c in range(2):
                send[r * 8 + 2 * n + c, 0] = out[r * 64 : (r + 1) * 64, c * 128 : (c + 1) * 128]
    low = low_half((64, 128))
    for m in range(2):
        out = dot(d_scr[:, m * 512 : (m + 1) * 512], a_scr[...], 0, 0)
        for r in range(4):
            for c in range(8):
                lanes = slice(c * 128, (c + 1) * 128)
                send[(m * 4 + r) * 8 + c, 1] = jnp.where(
                    low, out[r * 128 : r * 128 + 64, lanes], out[r * 128 + 64 : (r + 1) * 128, lanes]
                ).astype(BF)


def weights_kernel(
    got, zn_cells, sl, gl, sr, gr, grad_gate, grad_out, dl_out, dr_out, send, acc, stage, scr
):
    @pl.when(pl.program_id(0) == 0)
    def _():
        acc[...] = jnp.zeros((512, 128), F32)

    rows = pl.ds(pl.multiple_of(pl.program_id(0) * STEP, STEP), STEP)
    for which, slope, bend, out in ((0, sl, gl, dl_out), (1, sr, gr, dr_out)):
        spread(got[:, which, rows], scr)
        grad = unpack(scr, 0, STEP)
        out[:128] = (grad * slope[...]).astype(BF)
        out[128:] = (grad * bend[...]).astype(BF)
        acc[which * 256 : (which + 1) * 256] += dot(out[...], zn_cells[...], 1, 0)

    @pl.when(pl.program_id(0) == pl.num_programs(0) - 1)
    def _():
        for t in range(6):
            if t < 4:
                tile = acc[t * 128 : (t + 1) * 128]
            else:
                tile = (grad_gate if t == 4 else grad_out)[...]
            for half in range(2):
                stage[pl.ds(2 * t + half, 64, stride=16), :] = tile[half * 64 : (half + 1) * 64]
        for t in range(12, 16):
            stage[pl.ds(t, 64, stride=16), :] = jnp.zeros((64, 128), F32)
        send[...] = stage[...].reshape(64, 16, 128).astype(BF)


def pair_kernel(pair, gain_ref, dl, dr, dg, w_left, w_right, w_gate, out):
    gain = column(gain_ref)
    for first, here in spans(ROWS):
        zhat, inverse = normalize(load_transposed(pair, first, ROWS))
        d_zn = (
            dot(w_left[...], dl[:, here], 1, 0)
            + dot(w_right[...], dr[:, here], 1, 0)
            + dot(w_gate[...], dg[:, here], 1, 0)
        )
        store_transposed(out, first, normalize_backward(d_zn * gain, zhat, inverse))


def sum_kernel(scale, got, send):
    total = got[0].astype(F32)
    for s in range(1, 64):
        total = total + got[s].astype(F32)
    send[...] = jnp.broadcast_to((total * scale).astype(BF)[None], send.shape)


def split_kernel(got, left, right, gate, out, stage):
    stage[...] = got[...].astype(F32).reshape(1024, 128)
    for t, (ref, lane) in enumerate(
        ((left, 0), (left, 128), (right, 0), (right, 128), (gate, 0), (out, 0))
    ):
        tile = jnp.concatenate(
            [stage[pl.ds(2 * t + half, 64, stride=16), :] for half in range(2)], axis=0
        )
        ref[:, lane : lane + 128] = jnp.transpose(tile) if t < 4 else tile


def call(kernel, grid, in_specs, out_specs, out_shape, scratch=(), cost=(10**9, 10**7)):
    return pl.pallas_call(
        kernel,
        grid=grid,
        in_specs=in_specs,
        out_specs=out_specs,
        out_shape=out_shape,
        scratch_shapes=list(scratch),
        cost_estimate=pl.CostEstimate(flops=cost[0], bytes_accessed=cost[1], transcendentals=0),
        compiler_params=pltpu.CompilerParams(vmem_limit_bytes=LIMIT),
    )


def whole(*dims):
    return pl.BlockSpec(dims, lambda *_: (0,) * len(dims))


def shape(dims, kind, space=None):
    return jax.ShapeDtypeStruct(dims, kind) if space is None else space(dims, kind)


def keep(value, space):
    return pltpu.with_memory_space_constraint(value, space)


def exchange(values):
    owners = values.shape[0]
    flat = values.reshape(owners, -1, 128)
    return lax.all_to_all(flat, AXES, 0, 0, tiled=True).reshape(values.shape)


def body(
    pair, length, ln_in_gain, ln_in_bias, w_left, w_right, w_gate,
    product_norm_gain, product_norm_bias, w_out, cotangent,
):
    tile_i, tile_j, chans = pair.shape
    total = tile_j * lax.axis_size("col")
    cells = tile_i * tile_j
    grid = (tile_i // STEP,)
    gain_in, bias_in = ln_in_gain.reshape(1, 128), ln_in_bias.reshape(1, 128)
    gain_p, bias_p = product_norm_gain.reshape(1, 128), product_norm_bias.reshape(1, 128)
    pair, cotangent = keep(pair, pltpu.HBM), keep(cotangent, pltpu.HBM)
    w_left, w_right, w_gate, w_out = (
        keep(w, pltpu.HBM) for w in (w_left, w_right, w_gate, w_out)
    )

    natural = pl.BlockSpec((STEP, 64, 128), lambda i: (i, 0, 0))
    chan_major = pl.BlockSpec((128, CELLS), lambda i: (0, i))
    chan_major2 = pl.BlockSpec((256, CELLS), lambda i: (0, i))
    cell_major = pl.BlockSpec((CELLS, 128), lambda i: (i, 0))
    single = pl.BlockSpec((64, STEP, 128), lambda i: (0, i, 0))
    double = pl.BlockSpec((64, 2, STEP, 128), lambda i: (0, 0, i, 0))
    direct = pl.BlockSpec(memory_space=pltpu.VMEM)
    scalar = pl.BlockSpec(memory_space=pltpu.SMEM)
    vec, wide, square = whole(1, 128), whole(128, 256), whole(128, 128)
    swap = pltpu.VMEM((64 * PITCH, 128), F32)
    near, far = pltpu.VMEM, pltpu.HBM
    b_cells = shape((128, cells), BF, far)
    f_square = shape((128, 128), F32, far)
    a_map, b_map = pltpu.VMEM((512, 1024), BF), pltpu.VMEM((1024, 1024), BF)

    send, zn = call(
        operands_kernel, grid,
        [natural, scalar, vec, vec, wide, wide],
        [direct, chan_major],
        [shape((64, 2, 64, 128), BF, near), b_cells],
        [swap] * 2,
    )(pair, length, gain_in, bias_in, w_left, w_right)
    zn = keep(zn, far)
    operands = keep(exchange(send), near)

    *factors, hat_grad, zn_cells = call(
        factors_kernel, grid,
        [chan_major, scalar, natural, vec, wide, wide, square, square],
        [chan_major] * 4 + [single, cell_major],
        [b_cells] * 4 + [shape((64, 64, 128), F32, far), shape((cells, 128), BF, far)],
        [swap],
    )(zn, length, cotangent, gain_p, w_left, w_right, w_gate, w_out)
    factors = [keep(f, far) for f in factors]

    product = call(
        product_kernel, (1,),
        [direct],
        pl.BlockSpec(memory_space=pltpu.HBM),
        shape((8, 8, 64, 128), BF, far),
        [a_map, b_map, pltpu.VMEM((8, 8, 64, 128), BF), pltpu.SemaphoreType.DMA((4,))],
    )(operands).reshape(64, 64, 128)

    product = keep(exchange(product), near)
    send = call(
        middle_kernel, grid,
        [direct, single],
        direct,
        shape((64, 64, 128), BF, near),
    )(product, keep(hat_grad, far))
    got = exchange(send)

    updated, d_gpre, grad_out, grad_gate = call(
        updated_kernel, grid,
        [single, chan_major, natural, vec, vec, square, square],
        [natural, chan_major, square, square],
        [shape(pair.shape, BF, far), b_cells, f_square, f_square],
        [swap],
    )(product, zn, cotangent, gain_p, bias_p, w_out, w_gate)

    send = call(
        product_grads_kernel, (1,),
        [direct, direct],
        whole(64, 2, 64, 128),
        shape((64, 2, 64, 128), BF, far),
        [a_map, b_map, a_map],
    )(keep(got, near), operands)

    d_left, d_right, terms = call(
        weights_kernel, grid,
        [direct, cell_major] + [chan_major] * 4 + [square, square],
        [chan_major2, chan_major2, whole(64, 16, 128)],
        [shape((256, cells), BF, far)] * 2 + [shape((64, 16, 128), BF, far)],
        [pltpu.VMEM((512, 128), F32), pltpu.VMEM((1024, 128), F32), swap],
    )(keep(exchange(send), near), keep(zn_cells, far), *factors, keep(grad_gate, far), keep(grad_out, far))
    shares = exchange(terms)

    d_pair = call(
        pair_kernel, grid,
        [natural, vec, chan_major2, chan_major2, chan_major, wide, wide, square],
        natural,
        shape(pair.shape, BF, far),
    )(pair, gain_in, keep(d_left, far), keep(d_right, far), keep(d_gpre, far), w_left, w_right, w_gate)

    summed = call(
        functools.partial(sum_kernel, 1.0 / total), (1,),
        [whole(64, 16, 128)], whole(64, 16, 128), shape((64, 16, 128), BF, far), cost=(10**6, 10**6),
    )(shares)
    sums = call(
        split_kernel, (1,),
        [whole(64, 16, 128)],
        [wide, wide, square, square],
        [shape((128, 256), F32)] * 2 + [shape((128, 128), F32)] * 2,
        [pltpu.VMEM((1024, 128), F32)],
        cost=(10**6, 10**6),
    )(exchange(summed))
    return (updated, d_pair, *sums)


def solution(mesh):
    in_specs = (
        P(("rep", "row"), "col", None),
        P("rep"),
        P(),
        P(),
        P(),
        P(),
        P(),
        P(),
        P(),
        P(),
        P(("rep", "row"), "col", None),
    )
    out_specs = (
        P(("rep", "row"), "col", None),
        P(("rep", "row"), "col", None),
        P("rep", None),
        P("rep", None),
        P("rep", None),
        P("rep", None),
    )
    return jax.shard_map(body, mesh=mesh, in_specs=in_specs, out_specs=out_specs, check_vma=False)
```

time: 176 us -> 173 us (0.983)
  waiting for transfers between devices: 40.7 us -> 38.2 us
    pallas_call x6, Pallas kernels: 29.5 us -> 26.9 us  [the longest x1 6.63 us: body(): call(weights_kernel, grid, [direct, cell_major] + [chan_major] * 4 + [squ...]
    all_to_all x3, waiting for transfers between devices: 40.7 us -> 38.2 us  [exchange(): return lax.all_to_all(flat, AXES, 0, 0, tiled=True).reshape(values.shape)]
  transfers between devices with their start and end apart: 3 -> 3, of which waited for: 3 -> 3; matrix products, arithmetic and copies ran while one was open for 0% -> 0% of each run, Pallas kernels for 9% -> 10%
where the time goes in v3:
time: 173 us; the launch traced here: 172 us
  blocking collectives  76.1 us (44%)
  Pallas kernels  40.9 us (24%)
  waiting for transfers between devices  38.2 us (22%)
  starting transfers between devices  14.1 us (8%)
    all_to_all x3, blocking collectives, exchange(): return lax.all_to_all(flat, AXES, 0, 0, tiled=True).reshape(values.shape)  76.1 us
    all_to_all x3, waiting for transfers between devices, exchange(): return lax.all_to_all(flat, AXES, 0, 0, tiled=True).reshape(values.shape)  38.2 us
    all_to_all x3, starting transfers between devices, exchange(): return lax.all_to_all(flat, AXES, 0, 0, tiled=True).reshape(values.shape)  14.1 us
    pallas_call x1, Pallas kernels, body(): call(factors_kernel, grid, [chan_major, scalar, natural, vec, wide, wide,...  6.72 us
    pallas_call x1, Pallas kernels, body(): call(weights_kernel, grid, [direct, cell_major] + [chan_major] * 4 + [squ...  6.63 us
    pallas_call x1, Pallas kernels, body(): call(pair_kernel, grid, [natural, vec, chan_major2, chan_major2, chan_maj...  5.63 us
    pallas_call x1, Pallas kernels, body(): call(updated_kernel, grid, [single, chan_major, natural, vec, vec, square...  5.49 us
    pallas_call x1, Pallas kernels, body(): call(operands_kernel, grid, [natural, scalar, vec, vec, wide, wide], [dir...  4.88 us
  transfers between devices with their start and end apart: 3, of which 3 were waited for; matrix products, arithmetic and copies ran while one was open for 0% of the time, Pallas kernels for 10%

profile of v3, /device:TPU:1, one launch (start us, length us, event | category | flops | bytes accessed | tf_op | source)
XLA Modules:
  0.0 172.0 jit_solution(7649558696442422295)
XLA Ops:
  1.3 0.0 copy-start
  1.3 0.6 copy-done
  1.9 0.7 copy-done.2
  2.6 4.9 %shard_map.154 = (bf16[64,2,64,128]{3,2,1,0:T(8,128)(2,1)S(1)}, bf16[128,4096]{1,0:T(8,128)(2,1)}) custom-call(bf16[64,64,128]{2,1,0:T(8,128)(2,1)} %pair.3, s32[1]{0:T(128)S(6)} %copy.17.length, f32[1,128]{1,0:T(1,128)S(1)} %bitcast.13, f32[1,128]{1,0:T(1,128)S(1)} %bitcast.15, bf16[128,256]{1,0:T(8,128)(2,1)} %w_left.5, bf16[128,256]{1,0:T(8,128)(2,1)} %w_right.5), custom_call_target="tpu_custom_call" | custom-call | flops 1000000000 | bytes 10000000 | tf_op jit(solution)/shard_map/pallas_call | solution.py:368
  7.5 39.2 %all_to_all.30 = bf16[64,128,128]{2,1,0:T(8,128)(2,1)S(1)} all-to-all(bf16[64,128,128]{2,1,0:T(8,128)(2,1)S(1)} %bitcast.12), channel_id=1, replica_groups=mesh['row'=8,'col'=8,'rep'=2] {'row','col'}, dimensions={0} | all-to-all | bytes 4194304 | tf_op jit(solution)/shard_map/all_to_all | solution.py:335
  46.7 2.3 %shard_map.155 = bf16[8,8,64,128]{3,2,1,0:T(8,128)(2,1)} custom-call(bf16[64,2,64,128]{3,2,1,0:T(8,128)(2,1)S(1)} %bitcast.10), custom_call_target="tpu_custom_call" | custom-call | flops 1000000000 | bytes 10000000 | tf_op jit(solution)/shard_map/pallas_call | solution.py:387
  49.0 5.0 %all-to-all-start.1 = ((bf16[64,64,128]{2,1,0:T(8,128)(2,1)}), bf16[64,64,128]{2,1,0:T(8,128)(2,1)S(1)}, u32[]{:S(2)}, u32[]{:S(2)}) async-start(bf16[64,64,128]{2,1,0:T(8,128)(2,1)} %bitcast.20), calls=%async_computation.1 | async-start | bytes 2097152 | tf_op jit(solution)/shard_map/all_to_all | solution.py:335
  54.0 0.0 copy-done.3
  54.0 6.7 %shard_map.157 = (bf16[128,4096]{1,0:T(8,128)(2,1)}, bf16[128,4096]{1,0:T(8,128)(2,1)}, bf16[128,4096]{1,0:T(8,128)(2,1)}, bf16[128,4096]{1,0:T(8,128)(2,1)}, f3...) custom-call(bf16[128,4096]{1,0:T(8,128)(2,1)} %get-tuple-element.26.zn_ref, s32[1]{0:T(128)S(6)} %copy.17.length, ...), custom_call_target="tpu_custom_call" | custom-call | flops 1000000000 | bytes 10000000 | tf_op jit(solution)/shard_map/pallas_call | solution.py:378
  60.7 11.2 %all-to-all-done.1.product.got = bf16[64,64,128]{2,1,0:T(8,128)(2,1)S(1)} async-done(((bf16[64,64,128]{2,1,0:T(8,128)(2,1)}), bf16[64,64,128]{2,1,0:T(8,128)(2,1)S(1)}, u32[]{:S(2)}, u32[]{:S(2)}) %all-to-all-start.1) | async-done | bytes 1048608 | tf_op jit(solution)/shard_map/all_to_all | solution.py:335
  71.9 3.6 %shard_map.158 = bf16[64,64,128]{2,1,0:T(8,128)(2,1)S(1)} custom-call(bf16[64,64,128]{2,1,0:T(8,128)(2,1)S(1)} %all-to-all-done.1.product.got, f32[64,64,128]{2,1,0:T(8,128)} %get-tuple-element.28.hat_grad), custom_call_target="tpu_custom_call" | custom-call | flops 1000000000 | bytes 10000000 | tf_op jit(solution)/shard_map/pallas_call | solution.py:396
  75.5 22.2 %all_to_all.31.got = bf16[64,64,128]{2,1,0:T(8,128)(2,1)S(1)} all-to-all(bf16[64,64,128]{2,1,0:T(8,128)(2,1)S(1)} %shard_map.158), channel_id=1, replica_groups=mesh['row'=8,'col'=8,'rep'=2] {'row','col'}, dimensions={0} | all-to-all | bytes 2097152 | tf_op jit(solution)/shard_map/all_to_all | solution.py:335
  97.7 4.0 %shard_map.159 = bf16[64,2,64,128]{3,2,1,0:T(8,128)(2,1)} custom-call(bf16[64,64,128]{2,1,0:T(8,128)(2,1)S(1)} %all_to_all.31.got, bf16[64,2,64,128]{3,2,1,0:T(8,128)(2,1)S(1)} %bitcast.11), custom_call_target="tpu_custom_call" | custom-call | flops 1000000000 | bytes 10000000 | tf_op jit(solution)/shard_map/pallas_call | solution.py:412
  101.7 4.6 %all-to-all-start.3 = ((bf16[64,128,128]{2,1,0:T(8,128)(2,1)}), bf16[64,128,128]{2,1,0:T(8,128)(2,1)S(1)}, u32[]{:S(2)}, u32[]{:S(2)}) async-start(bf16[64,128,128]{2,1,0:T(8,128)(2,1)} %bitcast.19), calls=%async_computation.3 | async-start | bytes 4194304 | tf_op jit(solution)/shard_map/all_to_all | solution.py:335
  106.3 0.0 copy-done.4
  106.3 5.5 %shard_map.156 = (bf16[64,64,128]{2,1,0:T(8,128)(2,1)}, bf16[128,4096]{1,0:T(8,128)(2,1)}, f32[128,128]{1,0:T(8,128)}, f32[128,128]{1,0:T(8,128)}) custom-call(bf16[64,64,128]{2,1,0:T(8,128)(2,1)S(1)} %all-to-all-done.1.product.got, bf16[128,4096]{1,0:T(8,128)(2,1)} %get-tuple-element.26.zn_ref, bf16[64,64,128]{2,1,0:T(8,128)(2,1)} %cot.3, ...), custom_call_target="tpu_custom_call" | custom-call | flops 1000000000 | bytes 10000000 | tf_op jit(solution)/shard_map/pallas_call | solution.py:404
  111.8 23.0 %all-to-all-done.3 = bf16[64,128,128]{2,1,0:T(8,128)(2,1)S(1)} async-done(((bf16[64,128,128]{2,1,0:T(8,128)(2,1)}), bf16[64,128,128]{2,1,0:T(8,128)(2,1)S(1)}, u32[]{:S(2)}, u32[]{:S(2)}) %all-to-all-start.3) | async-done | bytes 2097184 | tf_op jit(solution)/shard_map/all_to_all | solution.py:335
  134.8 6.6 %shard_map.160 = (bf16[256,4096]{1,0:T(8,128)(2,1)}, bf16[256,4096]{1,0:T(8,128)(2,1)}, bf16[64,16,128]{2,1,0:T(8,128)(2,1)}) custom-call(bf16[64,2,64,128]{3,2,1,0:T(8,128)(2,1)S(1)} %bitcast.9, bf16[4096,128]{1,0:T(8,128)(2,1)} %get-tuple-element.29.zn_cells, bf16[128,4096]{1,0:T(8,128)(2,1)} %get-tuple-element.30.sl, ...), custom_call_target="tpu_custom_call" | custom-call | flops 1000000000 | bytes 10000000 | tf_op jit(solution)/shard_map/pallas_call | solution.py:420
  141.4 14.7 %all_to_all.32.got = bf16[64,16,128]{2,1,0:T(8,128)(2,1)S(1)} all-to-all(bf16[64,16,128]{2,1,0:T(8,128)(2,1)} %get-tuple-element.39), channel_id=1, replica_groups=mesh['row'=8,'col'=8,'rep'=2] {'row','col'}, dimensions={0} | all-to-all | bytes 524288 | tf_op jit(solution)/shard_map/all_to_all | solution.py:335
  156.1 0.8 shard_map.162
  156.9 4.5 %all-to-all-start.5 = ((bf16[64,16,128]{2,1,0:T(8,128)(2,1)}), bf16[64,16,128]{2,1,0:T(8,128)(2,1)S(1)}, u32[]{:S(2)}, u32[]{:S(2)}) async-start(bf16[64,16,128]{2,1,0:T(8,128)(2,1)} %shard_map.162), calls=%async_computation.5 | async-start | bytes 524288 | tf_op jit(solution)/shard_map/all_to_all | solution.py:335
  161.4 5.6 %shard_map.161 = bf16[64,64,128]{2,1,0:T(8,128)(2,1)} custom-call(bf16[64,64,128]{2,1,0:T(8,128)(2,1)} %pair.3, f32[1,128]{1,0:T(1,128)S(1)} %bitcast.14, bf16[256,4096]{1,0:T(8,128)(2,1)} %get-tuple-element.36.dl, bf16[256,4096]{1,0:T(8,128)(2,1)} %get-tuple-element.37.dr, bf16[128,4096]{1,0:T(8,128)(2,1)} %get-tuple-element.38.dg, ...), custom_call_target="tpu_custom_call" | custom-call | flops 1000000000 | bytes 10000000 | tf_op jit(solution)/shard_map/pallas_call | solution.py:429
  167.0 4.0 %all-to-all-done.5.got = bf16[64,16,128]{2,1,0:T(8,128)(2,1)S(1)} async-done(((bf16[64,16,128]{2,1,0:T(8,128)(2,1)}), bf16[64,16,128]{2,1,0:T(8,128)(2,1)S(1)}, u32[]{:S(2)}, u32[]{:S(2)}) %all-to-all-start.5) | async-done | bytes 262176 | tf_op jit(solution)/shard_map/all_to_all | solution.py:335
  171.1 0.9 shard_map.163
  (5 shorter events, 0.0 us)
Async XLA Ops:
  1.3 0.7 copy-start
  1.9 0.7 copy-start.2
  46.7 7.3 %copy-start.3 = (f32[128]{0:T(128)S(1)}, f32[128]{0:T(128)}, u32[]{:S(2)}) copy-start(f32[128]{0:T(128)} %param.18) | copy-start | bytes 1540
  49.0 23.0 %all-to-all-start.1 = ((bf16[64,64,128]{2,1,0:T(8,128)(2,1)}), bf16[64,64,128]{2,1,0:T(8,128)(2,1)S(1)}, u32[]{:S(2)}, u32[]{:S(2)}) async-start(bf16[64,64,128]{2,1,0:T(8,128)(2,1)} %bitcast.20), calls=%async_computation.1 | async-start | bytes 2097152 | tf_op jit(solution)/shard_map/all_to_all | solution.py:335
  101.7 4.6 %copy-start.4 = (f32[128]{0:T(128)S(1)}, f32[128]{0:T(128)}, u32[]{:S(2)}) copy-start(f32[128]{0:T(128)} %param.19) | copy-start | bytes 1540
  101.7 33.1 %all-to-all-start.3 = ((bf16[64,128,128]{2,1,0:T(8,128)(2,1)}), bf16[64,128,128]{2,1,0:T(8,128)(2,1)S(1)}, u32[]{:S(2)}, u32[]{:S(2)}) async-start(bf16[64,128,128]{2,1,0:T(8,128)(2,1)} %bitcast.19), calls=%async_computation.3 | async-start | bytes 4194304 | tf_op jit(solution)/shard_map/all_to_all | solution.py:335
  134.8 26.6 %copy-start.1 = (f32[128]{0:T(128)S(1)}, f32[128]{0:T(128)}, u32[]{:S(2)}) copy-start(f32[128]{0:T(128)} %param.13) | copy-start | bytes 1540
  156.9 14.2 %all-to-all-start.5 = ((bf16[64,16,128]{2,1,0:T(8,128)(2,1)}), bf16[64,16,128]{2,1,0:T(8,128)(2,1)S(1)}, u32[]{:S(2)}, u32[]{:S(2)}) async-start(bf16[64,16,128]{2,1,0:T(8,128)(2,1)} %shard_map.162), calls=%async_computation.5 | async-start | bytes 524288 | tf_op jit(solution)/shard_map/all_to_all | solution.py:335

commit v4 on v3

--- a/solution.py
+++ b/solution.py
@@ -10,9 +10,9 @@
 AXES = ("row", "col")
 BF = jnp.bfloat16
 F32 = jnp.float32
-STEP = 16
+STEP = 32
 ROWS = 16
-PITCH = 17
+PITCH = 33
 CELLS = STEP * 64
 LIMIT = 32 * 1024 * 1024
 EPS = 1e-05
@@ -245,20 +245,23 @@
                 ).astype(BF)
 
 
+def cell_grads(got, which, slope, bend, scr):
+    rows = pl.ds(pl.multiple_of(pl.program_id(0) * STEP, STEP), STEP)
+    spread(got[:, which, rows], scr)
+    grad = unpack(scr, 0, STEP)
+    return jnp.concatenate([grad * slope[...], grad * bend[...]], axis=0).astype(BF)
+
+
 def weights_kernel(
-    got, zn_cells, sl, gl, sr, gr, grad_gate, grad_out, dl_out, dr_out, send, acc, stage, scr
+    got, zn_cells, sl, gl, sr, gr, grad_gate, grad_out, send, acc, stage, scr
 ):
     @pl.when(pl.program_id(0) == 0)
     def _():
         acc[...] = jnp.zeros((512, 128), F32)
 
-    rows = pl.ds(pl.multiple_of(pl.program_id(0) * STEP, STEP), STEP)
-    for which, slope, bend, out in ((0, sl, gl, dl_out), (1, sr, gr, dr_out)):
-        spread(got[:, which, rows], scr)
-        grad = unpack(scr, 0, STEP)
-        out[:128] = (grad * slope[...]).astype(BF)
-        out[128:] = (grad * bend[...]).astype(BF)
-        acc[which * 256 : (which + 1) * 256] += dot(out[...], zn_cells[...], 1, 0)
+    for which, slope, bend in ((0, sl, gl), (1, sr, gr)):
+        grads = cell_grads(got, which, slope, bend, scr)
+        acc[which * 256 : (which + 1) * 256] += dot(grads, zn_cells[...], 1, 0)
 
     @pl.when(pl.program_id(0) == pl.num_programs(0) - 1)
     def _():
@@ -274,13 +277,15 @@
         send[...] = stage[...].reshape(64, 16, 128).astype(BF)
 
 
-def pair_kernel(pair, gain_ref, dl, dr, dg, w_left, w_right, w_gate, out):
+def pair_kernel(pair, gain_ref, got, sl, gl, sr, gr, dg, w_left, w_right, w_gate, out, scr):
     gain = column(gain_ref)
+    d_left = cell_grads(got, 0, sl, gl, scr)
+    d_right = cell_grads(got, 1, sr, gr, scr)
     for first, here in spans(ROWS):
         zhat, inverse = normalize(load_transposed(pair, first, ROWS))
         d_zn = (
-            dot(w_left[...], dl[:, here], 1, 0)
-            + dot(w_right[...], dr[:, here], 1, 0)
+            dot(w_left[...], d_left[:, here], 1, 0)
+            + dot(w_right[...], d_right[:, here], 1, 0)
             + dot(w_gate[...], dg[:, here], 1, 0)
         )
         store_transposed(out, first, normalize_backward(d_zn * gain, zhat, inverse))
@@ -352,7 +357,6 @@
 
     natural = pl.BlockSpec((STEP, 64, 128), lambda i: (i, 0, 0))
     chan_major = pl.BlockSpec((128, CELLS), lambda i: (0, i))
-    chan_major2 = pl.BlockSpec((256, CELLS), lambda i: (0, i))
     cell_major = pl.BlockSpec((CELLS, 128), lambda i: (i, 0))
     single = pl.BlockSpec((64, STEP, 128), lambda i: (0, i, 0))
     double = pl.BlockSpec((64, 2, STEP, 128), lambda i: (0, 0, i, 0))
@@ -417,21 +421,23 @@
         [a_map, b_map, a_map],
     )(keep(got, near), operands)
 
-    d_left, d_right, terms = call(
+    grads = keep(exchange(send), near)
+    terms = call(
         weights_kernel, grid,
         [direct, cell_major] + [chan_major] * 4 + [square, square],
-        [chan_major2, chan_major2, whole(64, 16, 128)],
-        [shape((256, cells), BF, far)] * 2 + [shape((64, 16, 128), BF, far)],
+        whole(64, 16, 128),
+        shape((64, 16, 128), BF, far),
         [pltpu.VMEM((512, 128), F32), pltpu.VMEM((1024, 128), F32), swap],
-    )(keep(exchange(send), near), keep(zn_cells, far), *factors, keep(grad_gate, far), keep(grad_out, far))
+    )(grads, keep(zn_cells, far), *factors, keep(grad_gate, far), keep(grad_out, far))
     shares = exchange(terms)
 
     d_pair = call(
         pair_kernel, grid,
-        [natural, vec, chan_major2, chan_major2, chan_major, wide, wide, square],
+        [natural, vec, direct] + [chan_major] * 5 + [wide, wide, square],
         natural,
         shape(pair.shape, BF, far),
-    )(pair, gain_in, keep(d_left, far), keep(d_right, far), keep(d_gpre, far), w_left, w_right, w_gate)
+        [swap],
+    )(pair, gain_in, grads, *factors, keep(d_gpre, far), w_left, w_right, w_gate)
 
     summed = call(
         functools.partial(sum_kernel, 1.0 / total), (1,),

time: 173 us -> 170 us (0.983)
  Pallas kernels: 40.9 us -> 38.9 us
  transfers between devices with their start and end apart: 3 -> 3, of which waited for: 3 -> 3; matrix products, arithmetic and copies ran while one was open for 0% -> 0% of each run, Pallas kernels for 10% -> 11%
where the time goes in v4:
time: 170 us; the launch traced here: 169 us
  blocking collectives  76.1 us (45%)
  Pallas kernels  38.9 us (23%)
  waiting for transfers between devices  37.4 us (22%)
  starting transfers between devices  14.1 us (8%)
    all_to_all x3, blocking collectives, exchange(): return lax.all_to_all(flat, AXES, 0, 0, tiled=True).reshape(values.shape)  76.1 us
    all_to_all x3, waiting for transfers between devices, exchange(): return lax.all_to_all(flat, AXES, 0, 0, tiled=True).reshape(values.shape)  37.4 us
    all_to_all x3, starting transfers between devices, exchange(): return lax.all_to_all(flat, AXES, 0, 0, tiled=True).reshape(values.shape)  14.1 us
    pallas_call x1, Pallas kernels, body(): call(pair_kernel, grid, [natural, vec, direct] + [chan_major] * 5 + [wide...  6.89 us
    pallas_call x1, Pallas kernels, body(): call(factors_kernel, grid, [chan_major, scalar, natural, vec, wide, wide,...  6.73 us
    pallas_call x1, Pallas kernels, body(): call(weights_kernel, grid, [direct, cell_major] + [chan_major] * 4 + [squ...  5.35 us
    pallas_call x1, Pallas kernels, body(): call(updated_kernel, grid, [single, chan_major, natural, vec, vec, square...  5.06 us
    pallas_call x1, Pallas kernels, body(): call(operands_kernel, grid, [natural, scalar, vec, vec, wide, wide], [dir...  4.11 us
  transfers between devices with their start and end apart: 3, of which 3 were waited for; matrix products, arithmetic and copies ran while one was open for 0% of the time, Pallas kernels for 11%

profile of v4, /device:TPU:1, one launch (start us, length us, event | category | flops | bytes accessed | tf_op | source)
XLA Modules:
  0.0 169.1 jit_solution(16690030611029833682)
XLA Ops:
  1.3 0.0 copy-start
  1.3 0.6 copy-done
  1.9 0.7 copy-done.2
  2.6 4.1 %shard_map.154 = (bf16[64,2,64,128]{3,2,1,0:T(8,128)(2,1)S(1)}, bf16[128,4096]{1,0:T(8,128)(2,1)}) custom-call(bf16[64,64,128]{2,1,0:T(8,128)(2,1)} %pair.3, s32[1]{0:T(128)S(6)} %copy.17.length, f32[1,128]{1,0:T(1,128)S(1)} %bitcast.14, f32[1,128]{1,0:T(1,128)S(1)} %bitcast.16, bf16[128,256]{1,0:T(8,128)(2,1)} %w_left.5, bf16[128,256]{1,0:T(8,128)(2,1)} %w_right.5), custom_call_target="tpu_custom_call" | custom-call | flops 1000000000 | bytes 10000000 | tf_op jit(solution)/shard_map/pallas_call | solution.py:372
  6.7 39.2 %all_to_all.30 = bf16[64,128,128]{2,1,0:T(8,128)(2,1)S(1)} all-to-all(bf16[64,128,128]{2,1,0:T(8,128)(2,1)S(1)} %bitcast.13), channel_id=1, replica_groups=mesh['row'=8,'col'=8,'rep'=2] {'row','col'}, dimensions={0} | all-to-all | bytes 4194304 | tf_op jit(solution)/shard_map/all_to_all | solution.py:340
  45.9 2.3 %shard_map.155 = bf16[8,8,64,128]{3,2,1,0:T(8,128)(2,1)} custom-call(bf16[64,2,64,128]{3,2,1,0:T(8,128)(2,1)S(1)} %bitcast.11), custom_call_target="tpu_custom_call" | custom-call | flops 1000000000 | bytes 10000000 | tf_op jit(solution)/shard_map/pallas_call | solution.py:391
  48.2 5.0 %all-to-all-start.1 = ((bf16[64,64,128]{2,1,0:T(8,128)(2,1)}), bf16[64,64,128]{2,1,0:T(8,128)(2,1)S(1)}, u32[]{:S(2)}, u32[]{:S(2)}) async-start(bf16[64,64,128]{2,1,0:T(8,128)(2,1)} %bitcast.21), calls=%async_computation.1 | async-start | bytes 2097152 | tf_op jit(solution)/shard_map/all_to_all | solution.py:340
  53.2 0.0 copy-done.3
  53.2 6.7 %shard_map.157 = (bf16[128,4096]{1,0:T(8,128)(2,1)}, bf16[128,4096]{1,0:T(8,128)(2,1)}, bf16[128,4096]{1,0:T(8,128)(2,1)}, bf16[128,4096]{1,0:T(8,128)(2,1)}, f3...) custom-call(bf16[128,4096]{1,0:T(8,128)(2,1)} %get-tuple-element.23.zn_ref, s32[1]{0:T(128)S(6)} %copy.17.length, ...), custom_call_target="tpu_custom_call" | custom-call | flops 1000000000 | bytes 10000000 | tf_op jit(solution)/shard_map/pallas_call | solution.py:382
  59.9 11.2 %all-to-all-done.1.product.got = bf16[64,64,128]{2,1,0:T(8,128)(2,1)S(1)} async-done(((bf16[64,64,128]{2,1,0:T(8,128)(2,1)}), bf16[64,64,128]{2,1,0:T(8,128)(2,1)S(1)}, u32[]{:S(2)}, u32[]{:S(2)}) %all-to-all-start.1) | async-done | bytes 1048608 | tf_op jit(solution)/shard_map/all_to_all | solution.py:340
  71.1 2.9 %shard_map.158 = bf16[64,64,128]{2,1,0:T(8,128)(2,1)S(1)} custom-call(bf16[64,64,128]{2,1,0:T(8,128)(2,1)S(1)} %all-to-all-done.1.product.got, f32[64,64,128]{2,1,0:T(8,128)} %get-tuple-element.25.hat_grad), custom_call_target="tpu_custom_call" | custom-call | flops 1000000000 | bytes 10000000 | tf_op jit(solution)/shard_map/pallas_call | solution.py:400
  74.0 22.2 %all_to_all.31.got = bf16[64,64,128]{2,1,0:T(8,128)(2,1)S(1)} all-to-all(bf16[64,64,128]{2,1,0:T(8,128)(2,1)S(1)} %shard_map.158), channel_id=1, replica_groups=mesh['row'=8,'col'=8,'rep'=2] {'row','col'}, dimensions={0} | all-to-all | bytes 2097152 | tf_op jit(solution)/shard_map/all_to_all | solution.py:340
  96.2 4.0 %shard_map.159 = bf16[64,2,64,128]{3,2,1,0:T(8,128)(2,1)} custom-call(bf16[64,64,128]{2,1,0:T(8,128)(2,1)S(1)} %all_to_all.31.got, bf16[64,2,64,128]{3,2,1,0:T(8,128)(2,1)S(1)} %bitcast.12), custom_call_target="tpu_custom_call" | custom-call | flops 1000000000 | bytes 10000000 | tf_op jit(solution)/shard_map/pallas_call | solution.py:416
  100.2 4.6 %all-to-all-start.3 = ((bf16[64,128,128]{2,1,0:T(8,128)(2,1)}), bf16[64,128,128]{2,1,0:T(8,128)(2,1)S(1)}, u32[]{:S(2)}, u32[]{:S(2)}) async-start(bf16[64,128,128]{2,1,0:T(8,128)(2,1)} %bitcast.20), calls=%async_computation.3 | async-start | bytes 4194304 | tf_op jit(solution)/shard_map/all_to_all | solution.py:340
  104.8 0.0 copy-done.4
  104.8 5.1 %shard_map.156 = (bf16[64,64,128]{2,1,0:T(8,128)(2,1)}, bf16[128,4096]{1,0:T(8,128)(2,1)}, f32[128,128]{1,0:T(8,128)}, f32[128,128]{1,0:T(8,128)}) custom-call(bf16[64,64,128]{2,1,0:T(8,128)(2,1)S(1)} %all-to-all-done.1.product.got, bf16[128,4096]{1,0:T(8,128)(2,1)} %get-tuple-element.23.zn_ref, bf16[64,64,128]{2,1,0:T(8,128)(2,1)} %cot.3, ...), custom_call_target="tpu_custom_call" | custom-call | flops 1000000000 | bytes 10000000 | tf_op jit(solution)/shard_map/pallas_call | solution.py:408
  109.8 23.4 %all-to-all-done.3 = bf16[64,128,128]{2,1,0:T(8,128)(2,1)S(1)} async-done(((bf16[64,128,128]{2,1,0:T(8,128)(2,1)}), bf16[64,128,128]{2,1,0:T(8,128)(2,1)S(1)}, u32[]{:S(2)}, u32[]{:S(2)}) %all-to-all-start.3) | async-done | bytes 2097184 | tf_op jit(solution)/shard_map/all_to_all | solution.py:340
  133.2 5.4 %shard_map.161 = bf16[64,16,128]{2,1,0:T(8,128)(2,1)} custom-call(bf16[64,2,64,128]{3,2,1,0:T(8,128)(2,1)S(1)} %bitcast.9, bf16[4096,128]{1,0:T(8,128)(2,1)} %get-tuple-element.31.zn_cells, bf16[128,4096]{1,0:T(8,128)(2,1)} %get-tuple-element.26.sl, bf16[128,4096]{1,0:T(8,128)(2,1)} %get-tuple-element.27.gl, bf16[128,4096]{1,0:T(8,128)(2,1)} %get-tuple-element.28.sr, ...), custom_call_target="tpu_custom_call" | custom-call | flops 1000000000 | bytes 10000000 | tf_op jit(solution)/shard_map/pallas_call | solution.py:425
  138.6 14.7 %all_to_all.32.got = bf16[64,16,128]{2,1,0:T(8,128)(2,1)S(1)} all-to-all(bf16[64,16,128]{2,1,0:T(8,128)(2,1)} %shard_map.161), channel_id=1, replica_groups=mesh['row'=8,'col'=8,'rep'=2] {'row','col'}, dimensions={0} | all-to-all | bytes 524288 | tf_op jit(solution)/shard_map/all_to_all | solution.py:340
  153.3 0.8 shard_map.162
  154.0 4.5 %all-to-all-start.5 = ((bf16[64,16,128]{2,1,0:T(8,128)(2,1)}), bf16[64,16,128]{2,1,0:T(8,128)(2,1)S(1)}, u32[]{:S(2)}, u32[]{:S(2)}) async-start(bf16[64,16,128]{2,1,0:T(8,128)(2,1)} %shard_map.162), calls=%async_computation.5 | async-start | bytes 524288 | tf_op jit(solution)/shard_map/all_to_all | solution.py:340
  158.6 6.9 %shard_map.160 = bf16[64,64,128]{2,1,0:T(8,128)(2,1)} custom-call(bf16[64,64,128]{2,1,0:T(8,128)(2,1)} %pair.3, f32[1,128]{1,0:T(1,128)S(1)} %bitcast.15, bf16[64,2,64,128]{3,2,1,0:T(8,128)(2,1)S(1)} %bitcast.10, bf16[128,4096]{1,0:T(8,128)(2,1)} %get-tuple-element.26.sl, bf16[128,4096]{1,0:T(8,128)(2,1)} %get-tuple-element.27.gl, ...), custom_call_target="tpu_custom_call" | custom-call | flops 1000000000 | bytes 10000000 | tf_op jit(solution)/shard_map/pallas_call | solution.py:434
  165.5 2.8 %all-to-all-done.5.got = bf16[64,16,128]{2,1,0:T(8,128)(2,1)S(1)} async-done(((bf16[64,16,128]{2,1,0:T(8,128)(2,1)}), bf16[64,16,128]{2,1,0:T(8,128)(2,1)S(1)}, u32[]{:S(2)}, u32[]{:S(2)}) %all-to-all-start.5) | async-done | bytes 262176 | tf_op jit(solution)/shard_map/all_to_all | solution.py:340
  168.2 0.9 shard_map.163
  (5 shorter events, 0.0 us)
Async XLA Ops:
  1.3 0.7 copy-start
  1.9 0.7 copy-start.2
  45.9 7.3 %copy-start.3 = (f32[128]{0:T(128)S(1)}, f32[128]{0:T(128)}, u32[]{:S(2)}) copy-start(f32[128]{0:T(128)} %param.18) | copy-start | bytes 1540
  48.2 23.0 %all-to-all-start.1 = ((bf16[64,64,128]{2,1,0:T(8,128)(2,1)}), bf16[64,64,128]{2,1,0:T(8,128)(2,1)S(1)}, u32[]{:S(2)}, u32[]{:S(2)}) async-start(bf16[64,64,128]{2,1,0:T(8,128)(2,1)} %bitcast.21), calls=%async_computation.1 | async-start | bytes 2097152 | tf_op jit(solution)/shard_map/all_to_all | solution.py:340
  100.2 4.6 %copy-start.4 = (f32[128]{0:T(128)S(1)}, f32[128]{0:T(128)}, u32[]{:S(2)}) copy-start(f32[128]{0:T(128)} %param.19) | copy-start | bytes 1540
  100.2 33.1 %all-to-all-start.3 = ((bf16[64,128,128]{2,1,0:T(8,128)(2,1)}), bf16[64,128,128]{2,1,0:T(8,128)(2,1)S(1)}, u32[]{:S(2)}, u32[]{:S(2)}) async-start(bf16[64,128,128]{2,1,0:T(8,128)(2,1)} %bitcast.20), calls=%async_computation.3 | async-start | bytes 4194304 | tf_op jit(solution)/shard_map/all_to_all | solution.py:340
  133.2 25.3 %copy-start.1 = (f32[128]{0:T(128)S(1)}, f32[128]{0:T(128)}, u32[]{:S(2)}) copy-start(f32[128]{0:T(128)} %param.13) | copy-start | bytes 1540
  154.0 14.2 %all-to-all-start.5 = ((bf16[64,16,128]{2,1,0:T(8,128)(2,1)}), bf16[64,16,128]{2,1,0:T(8,128)(2,1)S(1)}, u32[]{:S(2)}, u32[]{:S(2)}) async-start(bf16[64,16,128]{2,1,0:T(8,128)(2,1)} %shard_map.162), calls=%async_computation.5 | async-start | bytes 524288 | tf_op jit(solution)/shard_map/all_to_all | solution.py:340

commit v5 on v4

--- a/solution.py
+++ b/solution.py
@@ -13,6 +13,7 @@
 STEP = 32
 ROWS = 16
 PITCH = 33
+PITCH_16 = 17
 CELLS = STEP * 64
 LIMIT = 32 * 1024 * 1024
 EPS = 1e-05
@@ -121,7 +122,7 @@
 
 def factors_kernel(
     zn_ref, length, cot, gain_ref, w_left, w_right, w_gate, w_out,
-    sl, gl, sr, gr, hat_grad, zn_cells, scr,
+    factors, hat_grad, zn_cells, scr,
 ):
     gain = column(gain_ref)
     for first, here in spans(ROWS):
@@ -131,11 +132,11 @@
         gate = sigmoid(dot(w_gate[...], zn, 0, 0))
         d_proj = (load_transposed(cot, first, ROWS) * gate).astype(BF)
         pack(dot(w_out[...], d_proj, 1, 0) * gain, first, scr)
-        for weights, slope, bend in ((w_left, sl, gl), (w_right, sr, gr)):
+        for which, weights in enumerate((w_left, w_right)):
             value = dot(weights[...], zn, 0, 0)
             sigma = sigmoid(value[128:])
-            slope[:, here] = (mask * sigma).astype(BF)
-            bend[:, here] = (mask * value[:128] * sigma * (1.0 - sigma)).astype(BF)
+            factors[which * 256 : which * 256 + 128, here] = (mask * sigma).astype(BF)
+            factors[which * 256 + 128 : which * 256 + 256, here] = (mask * value[:128] * sigma * (1.0 - sigma)).astype(BF)
     hat_grad[...] = packed(scr, F32)
 
 
@@ -223,7 +224,11 @@
         grad_gate[...] += dot(zn, d_gpre, 1, 1)
 
 
-def product_grads_kernel(got, operands_ref, send, a_scr, b_scr, d_scr):
+def product_grads_kernel(got, operands_ref, send, a_scr, b_scr, d_scr, out_scr, sems):
+    def copy(which):
+        part = (slice(None), which)
+        return pltpu.make_async_copy(out_scr.at[part], send.at[part], sems.at[which])
+
     gather_map(operands_ref, 0, a_scr)
     double_rows(operands_ref, 1, b_scr)
     for r in range(8):
@@ -233,34 +238,40 @@
         out = dot(d_scr[...], b_scr[:, n * 256 : (n + 1) * 256], 1, 0).astype(BF)
         for r in range(8):
             for c in range(2):
-                send[r * 8 + 2 * n + c, 0] = out[r * 64 : (r + 1) * 64, c * 128 : (c + 1) * 128]
+                out_scr[r * 8 + 2 * n + c, 0] = out[r * 64 : (r + 1) * 64, c * 128 : (c + 1) * 128]
+    copy(0).start()
     low = low_half((64, 128))
     for m in range(2):
         out = dot(d_scr[:, m * 512 : (m + 1) * 512], a_scr[...], 0, 0)
         for r in range(4):
             for c in range(8):
                 lanes = slice(c * 128, (c + 1) * 128)
-                send[(m * 4 + r) * 8 + c, 1] = jnp.where(
+                out_scr[(m * 4 + r) * 8 + c, 1] = jnp.where(
                     low, out[r * 128 : r * 128 + 64, lanes], out[r * 128 + 64 : (r + 1) * 128, lanes]
                 ).astype(BF)
-
-
-def cell_grads(got, which, slope, bend, scr):
+    copy(1).start()
+    copy(0).wait()
+    copy(1).wait()
+
+
+def cell_grads(got, which, factors, scr):
     rows = pl.ds(pl.multiple_of(pl.program_id(0) * STEP, STEP), STEP)
     spread(got[:, which, rows], scr)
     grad = unpack(scr, 0, STEP)
-    return jnp.concatenate([grad * slope[...], grad * bend[...]], axis=0).astype(BF)
+    slope = factors[which * 256 : which * 256 + 128]
+    bend = factors[which * 256 + 128 : which * 256 + 256]
+    return jnp.concatenate([grad * slope, grad * bend], axis=0).astype(BF)
 
 
 def weights_kernel(
-    got, zn_cells, sl, gl, sr, gr, grad_gate, grad_out, send, acc, stage, scr
+    got, zn_cells, factors, grad_gate, grad_out, send, acc, stage, scr
 ):
     @pl.when(pl.program_id(0) == 0)
     def _():
         acc[...] = jnp.zeros((512, 128), F32)
 
-    for which, slope, bend in ((0, sl, gl), (1, sr, gr)):
-        grads = cell_grads(got, which, slope, bend, scr)
+    for which in range(2):
+        grads = cell_grads(got, which, factors, scr)
         acc[which * 256 : (which + 1) * 256] += dot(grads, zn_cells[...], 1, 0)
 
     @pl.when(pl.program_id(0) == pl.num_programs(0) - 1)
@@ -271,16 +282,16 @@
             else:
                 tile = (grad_gate if t == 4 else grad_out)[...]
             for half in range(2):
-                stage[pl.ds(2 * t + half, 64, stride=16), :] = tile[half * 64 : (half + 1) * 64]
+                stage[pl.ds(2 * t + half, 64, stride=PITCH_16), :] = tile[half * 64 : (half + 1) * 64]
         for t in range(12, 16):
-            stage[pl.ds(t, 64, stride=16), :] = jnp.zeros((64, 128), F32)
-        send[...] = stage[...].reshape(64, 16, 128).astype(BF)
-
-
-def pair_kernel(pair, gain_ref, got, sl, gl, sr, gr, dg, w_left, w_right, w_gate, out, scr):
+            stage[pl.ds(t, 64, stride=PITCH_16), :] = jnp.zeros((64, 128), F32)
+        send[...] = jnp.stack([stage[d * PITCH_16 : d * PITCH_16 + 16] for d in range(64)]).astype(BF)
+
+
+def pair_kernel(pair, gain_ref, got, factors, dg, w_left, w_right, w_gate, out, scr):
     gain = column(gain_ref)
-    d_left = cell_grads(got, 0, sl, gl, scr)
-    d_right = cell_grads(got, 1, sr, gr, scr)
+    d_left = cell_grads(got, 0, factors, scr)
+    d_right = cell_grads(got, 1, factors, scr)
     for first, here in spans(ROWS):
         zhat, inverse = normalize(load_transposed(pair, first, ROWS))
         d_zn = (
@@ -299,12 +310,14 @@
 
 
 def split_kernel(got, left, right, gate, out, stage):
-    stage[...] = got[...].astype(F32).reshape(1024, 128)
+    wide = got[...].astype(F32)
+    for d in range(64):
+        stage[d * PITCH_16 : d * PITCH_16 + 16] = wide[d]
     for t, (ref, lane) in enumerate(
         ((left, 0), (left, 128), (right, 0), (right, 128), (gate, 0), (out, 0))
     ):
         tile = jnp.concatenate(
-            [stage[pl.ds(2 * t + half, 64, stride=16), :] for half in range(2)], axis=0
+            [stage[pl.ds(2 * t + half, 64, stride=PITCH_16), :] for half in range(2)], axis=0
         )
         ref[:, lane : lane + 128] = jnp.transpose(tile) if t < 4 else tile
 
@@ -357,6 +370,7 @@
 
     natural = pl.BlockSpec((STEP, 64, 128), lambda i: (i, 0, 0))
     chan_major = pl.BlockSpec((128, CELLS), lambda i: (0, i))
+    chan_major4 = pl.BlockSpec((512, CELLS), lambda i: (0, i))
     cell_major = pl.BlockSpec((CELLS, 128), lambda i: (i, 0))
     single = pl.BlockSpec((64, STEP, 128), lambda i: (0, i, 0))
     double = pl.BlockSpec((64, 2, STEP, 128), lambda i: (0, 0, i, 0))
@@ -379,14 +393,14 @@
     zn = keep(zn, far)
     operands = keep(exchange(send), near)
 
-    *factors, hat_grad, zn_cells = call(
+    factors, hat_grad, zn_cells = call(
         factors_kernel, grid,
         [chan_major, scalar, natural, vec, wide, wide, square, square],
-        [chan_major] * 4 + [single, cell_major],
-        [b_cells] * 4 + [shape((64, 64, 128), F32, far), shape((cells, 128), BF, far)],
+        [chan_major4, single, cell_major],
+        [shape((512, cells), BF, far), shape((64, 64, 128), F32, far), shape((cells, 128), BF, far)],
         [swap],
     )(zn, length, cotangent, gain_p, w_left, w_right, w_gate, w_out)
-    factors = [keep(f, far) for f in factors]
+    factors = keep(factors, far)
 
     product = call(
         product_kernel, (1,),
@@ -416,39 +430,39 @@
     send = call(
         product_grads_kernel, (1,),
         [direct, direct],
-        whole(64, 2, 64, 128),
+        pl.BlockSpec(memory_space=pltpu.HBM),
         shape((64, 2, 64, 128), BF, far),
-        [a_map, b_map, a_map],
+        [a_map, b_map, a_map, pltpu.VMEM((64, 2, 64, 128), BF), pltpu.SemaphoreType.DMA((2,))],
     )(keep(got, near), operands)
 
     grads = keep(exchange(send), near)
     terms = call(
         weights_kernel, grid,
-        [direct, cell_major] + [chan_major] * 4 + [square, square],
+        [direct, cell_major, chan_major4] + [square, square],
         whole(64, 16, 128),
         shape((64, 16, 128), BF, far),
-        [pltpu.VMEM((512, 128), F32), pltpu.VMEM((1024, 128), F32), swap],
-    )(grads, keep(zn_cells, far), *factors, keep(grad_gate, far), keep(grad_out, far))
+        [pltpu.VMEM((512, 128), F32), pltpu.VMEM((64 * PITCH_16, 128), F32), swap],
+    )(grads, keep(zn_cells, far), factors, keep(grad_gate, far), keep(grad_out, far))
     shares = exchange(terms)
 
     d_pair = call(
         pair_kernel, grid,
-        [natural, vec, direct] + [chan_major] * 5 + [wide, wide, square],
+        [natural, vec, direct, chan_major4, chan_major] + [wide, wide, square],
         natural,
         shape(pair.shape, BF, far),
         [swap],
-    )(pair, gain_in, grads, *factors, keep(d_gpre, far), w_left, w_right, w_gate)
+    )(pair, gain_in, grads, factors, keep(d_gpre, far), w_left, w_right, w_gate)
 
     summed = call(
         functools.partial(sum_kernel, 1.0 / total), (1,),
-        [whole(64, 16, 128)], whole(64, 16, 128), shape((64, 16, 128), BF, far), cost=(10**6, 10**6),
-    )(shares)
+        [direct], whole(64, 16, 128), shape((64, 16, 128), BF, far), cost=(10**6, 10**6),
+    )(keep(shares, near))
     sums = call(
         split_kernel, (1,),
         [whole(64, 16, 128)],
         [wide, wide, square, square],
         [shape((128, 256), F32)] * 2 + [shape((128, 128), F32)] * 2,
-        [pltpu.VMEM((1024, 128), F32)],
+        [pltpu.VMEM((64 * PITCH_16, 128), F32)],
         cost=(10**6, 10**6),
     )(exchange(summed))
     return (updated, d_pair, *sums)

time: 170 us -> 169 us (level)
  no operation moved by 1% of the time
where the time goes in v5:
time: 169 us; the launch traced here: 168 us
  blocking collectives  76.1 us (45%)
  Pallas kernels  38.8 us (23%)
  waiting for transfers between devices  36.9 us (22%)
  starting transfers between devices  14 us (8%)
    all_to_all x3, blocking collectives, exchange(): return lax.all_to_all(flat, AXES, 0, 0, tiled=True).reshape(values.shape)  76.1 us
    all_to_all x3, waiting for transfers between devices, exchange(): return lax.all_to_all(flat, AXES, 0, 0, tiled=True).reshape(values.shape)  36.9 us
    all_to_all x3, starting transfers between devices, exchange(): return lax.all_to_all(flat, AXES, 0, 0, tiled=True).reshape(values.shape)  14 us
    pallas_call x1, Pallas kernels, body(): call(pair_kernel, grid, [natural, vec, direct, chan_major4, chan_major] +...  7.14 us
    pallas_call x1, Pallas kernels, body(): call(factors_kernel, grid, [chan_major, scalar, natural, vec, wide, wide,...  6.98 us
    pallas_call x1, Pallas kernels, body(): call(updated_kernel, grid, [single, chan_major, natural, vec, vec, square...  5.06 us
    pallas_call x1, Pallas kernels, body(): call(weights_kernel, grid, [direct, cell_major, chan_major4] + [square, s...  4.98 us
    pallas_call x1, Pallas kernels, body(): call(operands_kernel, grid, [natural, scalar, vec, vec, wide, wide], [dir...  4.11 us
  transfers between devices with their start and end apart: 3, of which 3 were waited for; matrix products, arithmetic and copies ran while one was open for 0% of the time, Pallas kernels for 11%

profile of v5, /device:TPU:1, one launch (start us, length us, event | category | flops | bytes accessed | tf_op | source)
XLA Modules:
  0.0 168.4 jit_solution(7202648882500259259)
XLA Ops:
  1.3 0.0 copy-start
  1.3 0.6 copy-done
  1.9 0.7 copy-done.2
  2.6 4.1 %shard_map.154 = (bf16[64,2,64,128]{3,2,1,0:T(8,128)(2,1)S(1)}, bf16[128,4096]{1,0:T(8,128)(2,1)}) custom-call(bf16[64,64,128]{2,1,0:T(8,128)(2,1)} %pair.3, s32[1]{0:T(128)S(6)} %copy.17.length, f32[1,128]{1,0:T(1,128)S(1)} %bitcast.14, f32[1,128]{1,0:T(1,128)S(1)} %bitcast.16, bf16[128,256]{1,0:T(8,128)(2,1)} %w_left.5, bf16[128,256]{1,0:T(8,128)(2,1)} %w_right.5), custom_call_target="tpu_custom_call" | custom-call | flops 1000000000 | bytes 10000000 | tf_op jit(solution)/shard_map/pallas_call | solution.py:386
  6.7 39.2 %all_to_all.30 = bf16[64,128,128]{2,1,0:T(8,128)(2,1)S(1)} all-to-all(bf16[64,128,128]{2,1,0:T(8,128)(2,1)S(1)} %bitcast.13), channel_id=1, replica_groups=mesh['row'=8,'col'=8,'rep'=2] {'row','col'}, dimensions={0} | all-to-all | bytes 4194304 | tf_op jit(solution)/shard_map/all_to_all | solution.py:353
  45.9 2.3 %shard_map.155 = bf16[8,8,64,128]{3,2,1,0:T(8,128)(2,1)} custom-call(bf16[64,2,64,128]{3,2,1,0:T(8,128)(2,1)S(1)} %bitcast.11), custom_call_target="tpu_custom_call" | custom-call | flops 1000000000 | bytes 10000000 | tf_op jit(solution)/shard_map/pallas_call | solution.py:405
  48.2 5.0 %all-to-all-start.1 = ((bf16[64,64,128]{2,1,0:T(8,128)(2,1)}), bf16[64,64,128]{2,1,0:T(8,128)(2,1)S(1)}, u32[]{:S(2)}, u32[]{:S(2)}) async-start(bf16[64,64,128]{2,1,0:T(8,128)(2,1)} %bitcast.21), calls=%async_computation.1 | async-start | bytes 2097152 | tf_op jit(solution)/shard_map/all_to_all | solution.py:353
  53.2 0.0 copy-done.3
  53.2 7.0 %shard_map.157 = (bf16[512,4096]{1,0:T(8,128)(2,1)}, f32[64,64,128]{2,1,0:T(8,128)}, bf16[4096,128]{1,0:T(8,128)(2,1)}) custom-call(bf16[128,4096]{1,0:T(8,128)(2,1)} %get-tuple-element.20.zn_ref, s32[1]{0:T(128)S(6)} %copy.17.length, bf16[64,64,128]{2,1,0:T(8,128)(2,1)} %cot.3, f32[1,128]{1,0:T(1,128)S(1)} %bitcast.17, bf16[128,256]{1,0:T(8,128)(2,1)} %w_left.5, ...), custom_call_target="tpu_custom_call" | custom-call | flops 1000000000 | bytes 10000000 | tf_op jit(solution)/shard_map/pallas_call | solution.py:396
  60.2 11.0 %all-to-all-done.1.product.got = bf16[64,64,128]{2,1,0:T(8,128)(2,1)S(1)} async-done(((bf16[64,64,128]{2,1,0:T(8,128)(2,1)}), bf16[64,64,128]{2,1,0:T(8,128)(2,1)S(1)}, u32[]{:S(2)}, u32[]{:S(2)}) %all-to-all-start.1) | async-done | bytes 1048608 | tf_op jit(solution)/shard_map/all_to_all | solution.py:353
  71.2 2.9 %shard_map.158 = bf16[64,64,128]{2,1,0:T(8,128)(2,1)S(1)} custom-call(bf16[64,64,128]{2,1,0:T(8,128)(2,1)S(1)} %all-to-all-done.1.product.got, f32[64,64,128]{2,1,0:T(8,128)} %get-tuple-element.22.hat_grad), custom_call_target="tpu_custom_call" | custom-call | flops 1000000000 | bytes 10000000 | tf_op jit(solution)/shard_map/pallas_call | solution.py:414
  74.0 22.2 %all_to_all.31.got = bf16[64,64,128]{2,1,0:T(8,128)(2,1)S(1)} all-to-all(bf16[64,64,128]{2,1,0:T(8,128)(2,1)S(1)} %shard_map.158), channel_id=1, replica_groups=mesh['row'=8,'col'=8,'rep'=2] {'row','col'}, dimensions={0} | all-to-all | bytes 2097152 | tf_op jit(solution)/shard_map/all_to_all | solution.py:353
  96.2 3.7 %shard_map.159 = bf16[64,2,64,128]{3,2,1,0:T(8,128)(2,1)} custom-call(bf16[64,64,128]{2,1,0:T(8,128)(2,1)S(1)} %all_to_all.31.got, bf16[64,2,64,128]{3,2,1,0:T(8,128)(2,1)S(1)} %bitcast.12), custom_call_target="tpu_custom_call" | custom-call | flops 1000000000 | bytes 10000000 | tf_op jit(solution)/shard_map/pallas_call | solution.py:430
  99.9 0.0 copy-start.4
  99.9 4.5 %all-to-all-start.3 = ((bf16[64,128,128]{2,1,0:T(8,128)(2,1)}), bf16[64,128,128]{2,1,0:T(8,128)(2,1)S(1)}, u32[]{:S(2)}, u32[]{:S(2)}) async-start(bf16[64,128,128]{2,1,0:T(8,128)(2,1)} %bitcast.20), calls=%async_computation.3 | async-start | bytes 4194304 | tf_op jit(solution)/shard_map/all_to_all | solution.py:353
  104.4 5.1 %shard_map.156 = (bf16[64,64,128]{2,1,0:T(8,128)(2,1)}, bf16[128,4096]{1,0:T(8,128)(2,1)}, f32[128,128]{1,0:T(8,128)}, f32[128,128]{1,0:T(8,128)}) custom-call(bf16[64,64,128]{2,1,0:T(8,128)(2,1)S(1)} %all-to-all-done.1.product.got, bf16[128,4096]{1,0:T(8,128)(2,1)} %get-tuple-element.20.zn_ref, bf16[64,64,128]{2,1,0:T(8,128)(2,1)} %cot.3, ...), custom_call_target="tpu_custom_call" | custom-call | flops 1000000000 | bytes 10000000 | tf_op jit(solution)/shard_map/pallas_call | solution.py:422
  109.5 23.4 %all-to-all-done.3 = bf16[64,128,128]{2,1,0:T(8,128)(2,1)S(1)} async-done(((bf16[64,128,128]{2,1,0:T(8,128)(2,1)}), bf16[64,128,128]{2,1,0:T(8,128)(2,1)S(1)}, u32[]{:S(2)}, u32[]{:S(2)}) %all-to-all-start.3) | async-done | bytes 2097184 | tf_op jit(solution)/shard_map/all_to_all | solution.py:353
  132.9 5.0 %shard_map.161 = bf16[64,16,128]{2,1,0:T(8,128)(2,1)} custom-call(bf16[64,2,64,128]{3,2,1,0:T(8,128)(2,1)S(1)} %bitcast.9, bf16[4096,128]{1,0:T(8,128)(2,1)} %get-tuple-element.25.zn_cells, bf16[512,4096]{1,0:T(8,128)(2,1)} %get-tuple-element.23.factors, f32[128,128]{1,0:T(8,128)} %get-tuple-element.26.grad_gate, f32[128,128]{1,0:T(8,128)} %get-tuple-element.27.grad_out), custom_call_target="tpu_custom_call" | custom-call | flops 1000000000 | bytes 10000000 | tf_op jit(solution)/shard_map/pallas_call | solution.py:439
  137.9 14.7 %all_to_all.32.got = bf16[64,16,128]{2,1,0:T(8,128)(2,1)S(1)} all-to-all(bf16[64,16,128]{2,1,0:T(8,128)(2,1)} %shard_map.161), channel_id=1, replica_groups=mesh['row'=8,'col'=8,'rep'=2] {'row','col'}, dimensions={0} | all-to-all | bytes 524288 | tf_op jit(solution)/shard_map/all_to_all | solution.py:353
  152.5 0.8 shard_map.162
  153.3 4.5 %all-to-all-start.5 = ((bf16[64,16,128]{2,1,0:T(8,128)(2,1)}), bf16[64,16,128]{2,1,0:T(8,128)(2,1)S(1)}, u32[]{:S(2)}, u32[]{:S(2)}) async-start(bf16[64,16,128]{2,1,0:T(8,128)(2,1)} %shard_map.162), calls=%async_computation.5 | async-start | bytes 524288 | tf_op jit(solution)/shard_map/all_to_all | solution.py:353
  157.9 7.1 %shard_map.160 = bf16[64,64,128]{2,1,0:T(8,128)(2,1)} custom-call(bf16[64,64,128]{2,1,0:T(8,128)(2,1)} %pair.3, f32[1,128]{1,0:T(1,128)S(1)} %bitcast.15, bf16[64,2,64,128]{3,2,1,0:T(8,128)(2,1)S(1)} %bitcast.10, bf16[512,4096]{1,0:T(8,128)(2,1)} %get-tuple-element.23.factors, bf16[128,4096]{1,0:T(8,128)(2,1)} %get-tuple-element.24.dg, ...), custom_call_target="tpu_custom_call" | custom-call | flops 1000000000 | bytes 10000000 | tf_op jit(solution)/shard_map/pallas_call | solution.py:448
  165.0 2.5 %all-to-all-done.5.got = bf16[64,16,128]{2,1,0:T(8,128)(2,1)S(1)} async-done(((bf16[64,16,128]{2,1,0:T(8,128)(2,1)}), bf16[64,16,128]{2,1,0:T(8,128)(2,1)S(1)}, u32[]{:S(2)}, u32[]{:S(2)}) %all-to-all-start.5) | async-done | bytes 262176 | tf_op jit(solution)/shard_map/all_to_all | solution.py:353
  167.5 0.9 shard_map.163
  (5 shorter events, 0.0 us)
Async XLA Ops:
  1.3 0.7 copy-start
  1.9 0.7 copy-start.2
  45.9 7.3 %copy-start.3 = (f32[128]{0:T(128)S(1)}, f32[128]{0:T(128)}, u32[]{:S(2)}) copy-start(f32[128]{0:T(128)} %param.18) | copy-start | bytes 1540
  48.2 22.9 %all-to-all-start.1 = ((bf16[64,64,128]{2,1,0:T(8,128)(2,1)}), bf16[64,64,128]{2,1,0:T(8,128)(2,1)S(1)}, u32[]{:S(2)}, u32[]{:S(2)}) async-start(bf16[64,64,128]{2,1,0:T(8,128)(2,1)} %bitcast.21), calls=%async_computation.1 | async-start | bytes 2097152 | tf_op jit(solution)/shard_map/all_to_all | solution.py:353
  99.9 4.5 %copy-start.4 = (f32[128]{0:T(128)S(1)}, f32[128]{0:T(128)}, u32[]{:S(2)}) copy-start(f32[128]{0:T(128)} %param.19) | copy-start | bytes 1540
  99.9 32.9 %all-to-all-start.3 = ((bf16[64,128,128]{2,1,0:T(8,128)(2,1)}), bf16[64,128,128]{2,1,0:T(8,128)(2,1)S(1)}, u32[]{:S(2)}, u32[]{:S(2)}) async-start(bf16[64,128,128]{2,1,0:T(8,128)(2,1)} %bitcast.20), calls=%async_computation.3 | async-start | bytes 4194304 | tf_op jit(solution)/shard_map/all_to_all | solution.py:353
  132.9 25.0 %copy-start.1 = (f32[128]{0:T(128)S(1)}, f32[128]{0:T(128)}, u32[]{:S(2)}) copy-start(f32[128]{0:T(128)} %param.13) | copy-start | bytes 1540
  153.3 14.2 %all-to-all-start.5 = ((bf16[64,16,128]{2,1,0:T(8,128)(2,1)}), bf16[64,16,128]{2,1,0:T(8,128)(2,1)S(1)}, u32[]{:S(2)}, u32[]{:S(2)}) async-start(bf16[64,16,128]{2,1,0:T(8,128)(2,1)} %shard_map.162), calls=%async_computation.5 | async-start | bytes 524288 | tf_op jit(solution)/shard_map/all_to_all | solution.py:353

commit v6 on v5

--- a/solution.py
+++ b/solution.py
@@ -377,7 +377,7 @@
     direct = pl.BlockSpec(memory_space=pltpu.VMEM)
     scalar = pl.BlockSpec(memory_space=pltpu.SMEM)
     vec, wide, square = whole(1, 128), whole(128, 256), whole(128, 128)
-    swap = pltpu.VMEM((64 * PITCH, 128), F32)
+    swap = pltpu.VMEM((66 * PITCH - 2, 128), F32)
     near, far = pltpu.VMEM, pltpu.HBM
     b_cells = shape((128, cells), BF, far)
     f_square = shape((128, 128), F32, far)
@@ -441,7 +441,7 @@
         [direct, cell_major, chan_major4] + [square, square],
         whole(64, 16, 128),
         shape((64, 16, 128), BF, far),
-        [pltpu.VMEM((512, 128), F32), pltpu.VMEM((64 * PITCH_16, 128), F32), swap],
+        [pltpu.VMEM((512, 128), F32), pltpu.VMEM((66 * PITCH_16 - 2, 128), F32), swap],
     )(grads, keep(zn_cells, far), factors, keep(grad_gate, far), keep(grad_out, far))
     shares = exchange(terms)
 
@@ -462,7 +462,7 @@
         [whole(64, 16, 128)],
         [wide, wide, square, square],
         [shape((128, 256), F32)] * 2 + [shape((128, 128), F32)] * 2,
-        [pltpu.VMEM((64 * PITCH_16, 128), F32)],
+        [pltpu.VMEM((66 * PITCH_16 - 2, 128), F32)],
         cost=(10**6, 10**6),
     )(exchange(summed))
     return (updated, d_pair, *sums)

time: 169 us -> 169 us (level)
  no operation moved by 1% of the time
where the time goes in v6:
time: 169 us; the launch traced here: 168 us
  blocking collectives  76 us (45%)
  Pallas kernels  38.8 us (23%)
  waiting for transfers between devices  36.9 us (22%)
  starting transfers between devices  14 us (8%)
    all_to_all x3, blocking collectives, exchange(): return lax.all_to_all(flat, AXES, 0, 0, tiled=True).reshape(values.shape)  76 us
    all_to_all x3, waiting for transfers between devices, exchange(): return lax.all_to_all(flat, AXES, 0, 0, tiled=True).reshape(values.shape)  36.9 us
    all_to_all x3, starting transfers between devices, exchange(): return lax.all_to_all(flat, AXES, 0, 0, tiled=True).reshape(values.shape)  14 us
    pallas_call x1, Pallas kernels, body(): call(pair_kernel, grid, [natural, vec, direct, chan_major4, chan_major] +...  7.13 us
    pallas_call x1, Pallas kernels, body(): call(factors_kernel, grid, [chan_major, scalar, natural, vec, wide, wide,...  6.98 us
    pallas_call x1, Pallas kernels, body(): call(updated_kernel, grid, [single, chan_major, natural, vec, vec, square...  5.06 us
    pallas_call x1, Pallas kernels, body(): call(weights_kernel, grid, [direct, cell_major, chan_major4] + [square, s...  4.98 us
    pallas_call x1, Pallas kernels, body(): call(operands_kernel, grid, [natural, scalar, vec, vec, wide, wide], [dir...  4.11 us
  transfers between devices with their start and end apart: 3, of which 3 were waited for; matrix products, arithmetic and copies ran while one was open for 0% of the time, Pallas kernels for 11%

profile of v6, /device:TPU:1, one launch (start us, length us, event | category | flops | bytes accessed | tf_op | source)
XLA Modules:
  0.0 168.4 jit_solution(3473747624882418677)
XLA Ops:
  1.3 0.0 copy-start
  1.3 0.6 copy-done
  1.9 0.7 copy-done.2
  2.6 4.1 %shard_map.154 = (bf16[64,2,64,128]{3,2,1,0:T(8,128)(2,1)S(1)}, bf16[128,4096]{1,0:T(8,128)(2,1)}) custom-call(bf16[64,64,128]{2,1,0:T(8,128)(2,1)} %pair.3, s32[1]{0:T(128)S(6)} %copy.17.length, f32[1,128]{1,0:T(1,128)S(1)} %bitcast.14, f32[1,128]{1,0:T(1,128)S(1)} %bitcast.16, bf16[128,256]{1,0:T(8,128)(2,1)} %w_left.5, bf16[128,256]{1,0:T(8,128)(2,1)} %w_right.5), custom_call_target="tpu_custom_call" | custom-call | flops 1000000000 | bytes 10000000 | tf_op jit(solution)/shard_map/pallas_call | solution.py:386
  6.7 39.2 %all_to_all.30 = bf16[64,128,128]{2,1,0:T(8,128)(2,1)S(1)} all-to-all(bf16[64,128,128]{2,1,0:T(8,128)(2,1)S(1)} %bitcast.13), channel_id=1, replica_groups=mesh['row'=8,'col'=8,'rep'=2] {'row','col'}, dimensions={0} | all-to-all | bytes 4194304 | tf_op jit(solution)/shard_map/all_to_all | solution.py:353
  45.9 2.3 %shard_map.155 = bf16[8,8,64,128]{3,2,1,0:T(8,128)(2,1)} custom-call(bf16[64,2,64,128]{3,2,1,0:T(8,128)(2,1)S(1)} %bitcast.11), custom_call_target="tpu_custom_call" | custom-call | flops 1000000000 | bytes 10000000 | tf_op jit(solution)/shard_map/pallas_call | solution.py:405
  48.2 5.0 %all-to-all-start.1 = ((bf16[64,64,128]{2,1,0:T(8,128)(2,1)}), bf16[64,64,128]{2,1,0:T(8,128)(2,1)S(1)}, u32[]{:S(2)}, u32[]{:S(2)}) async-start(bf16[64,64,128]{2,1,0:T(8,128)(2,1)} %bitcast.21), calls=%async_computation.1 | async-start | bytes 2097152 | tf_op jit(solution)/shard_map/all_to_all | solution.py:353
  53.2 7.0 %shard_map.157 = (bf16[512,4096]{1,0:T(8,128)(2,1)}, f32[64,64,128]{2,1,0:T(8,128)}, bf16[4096,128]{1,0:T(8,128)(2,1)}) custom-call(bf16[128,4096]{1,0:T(8,128)(2,1)} %get-tuple-element.20.zn_ref, s32[1]{0:T(128)S(6)} %copy.17.length, bf16[64,64,128]{2,1,0:T(8,128)(2,1)} %cot.3, f32[1,128]{1,0:T(1,128)S(1)} %bitcast.17, bf16[128,256]{1,0:T(8,128)(2,1)} %w_left.5, ...), custom_call_target="tpu_custom_call" | custom-call | flops 1000000000 | bytes 10000000 | tf_op jit(solution)/shard_map/pallas_call | solution.py:396
  60.2 11.0 %all-to-all-done.1.product.got = bf16[64,64,128]{2,1,0:T(8,128)(2,1)S(1)} async-done(((bf16[64,64,128]{2,1,0:T(8,128)(2,1)}), bf16[64,64,128]{2,1,0:T(8,128)(2,1)S(1)}, u32[]{:S(2)}, u32[]{:S(2)}) %all-to-all-start.1) | async-done | bytes 1048608 | tf_op jit(solution)/shard_map/all_to_all | solution.py:353
  71.2 2.9 %shard_map.158 = bf16[64,64,128]{2,1,0:T(8,128)(2,1)S(1)} custom-call(bf16[64,64,128]{2,1,0:T(8,128)(2,1)S(1)} %all-to-all-done.1.product.got, f32[64,64,128]{2,1,0:T(8,128)} %get-tuple-element.22.hat_grad), custom_call_target="tpu_custom_call" | custom-call | flops 1000000000 | bytes 10000000 | tf_op jit(solution)/shard_map/pallas_call | solution.py:414
  74.0 22.2 %all_to_all.31.got = bf16[64,64,128]{2,1,0:T(8,128)(2,1)S(1)} all-to-all(bf16[64,64,128]{2,1,0:T(8,128)(2,1)S(1)} %shard_map.158), channel_id=1, replica_groups=mesh['row'=8,'col'=8,'rep'=2] {'row','col'}, dimensions={0} | all-to-all | bytes 2097152 | tf_op jit(solution)/shard_map/all_to_all | solution.py:353
  96.2 3.7 %shard_map.159 = bf16[64,2,64,128]{3,2,1,0:T(8,128)(2,1)} custom-call(bf16[64,64,128]{2,1,0:T(8,128)(2,1)S(1)} %all_to_all.31.got, bf16[64,2,64,128]{3,2,1,0:T(8,128)(2,1)S(1)} %bitcast.12), custom_call_target="tpu_custom_call" | custom-call | flops 1000000000 | bytes 10000000 | tf_op jit(solution)/shard_map/pallas_call | solution.py:430
  99.9 0.0 copy-start.4
  99.9 4.5 %all-to-all-start.3 = ((bf16[64,128,128]{2,1,0:T(8,128)(2,1)}), bf16[64,128,128]{2,1,0:T(8,128)(2,1)S(1)}, u32[]{:S(2)}, u32[]{:S(2)}) async-start(bf16[64,128,128]{2,1,0:T(8,128)(2,1)} %bitcast.20), calls=%async_computation.3 | async-start | bytes 4194304 | tf_op jit(solution)/shard_map/all_to_all | solution.py:353
  104.4 0.0 copy-done.4
  104.4 5.1 %shard_map.156 = (bf16[64,64,128]{2,1,0:T(8,128)(2,1)}, bf16[128,4096]{1,0:T(8,128)(2,1)}, f32[128,128]{1,0:T(8,128)}, f32[128,128]{1,0:T(8,128)}) custom-call(bf16[64,64,128]{2,1,0:T(8,128)(2,1)S(1)} %all-to-all-done.1.product.got, bf16[128,4096]{1,0:T(8,128)(2,1)} %get-tuple-element.20.zn_ref, bf16[64,64,128]{2,1,0:T(8,128)(2,1)} %cot.3, ...), custom_call_target="tpu_custom_call" | custom-call | flops 1000000000 | bytes 10000000 | tf_op jit(solution)/shard_map/pallas_call | solution.py:422
  109.5 23.4 %all-to-all-done.3 = bf16[64,128,128]{2,1,0:T(8,128)(2,1)S(1)} async-done(((bf16[64,128,128]{2,1,0:T(8,128)(2,1)}), bf16[64,128,128]{2,1,0:T(8,128)(2,1)S(1)}, u32[]{:S(2)}, u32[]{:S(2)}) %all-to-all-start.3) | async-done | bytes 2097184 | tf_op jit(solution)/shard_map/all_to_all | solution.py:353
  132.9 5.0 %shard_map.161 = bf16[64,16,128]{2,1,0:T(8,128)(2,1)} custom-call(bf16[64,2,64,128]{3,2,1,0:T(8,128)(2,1)S(1)} %bitcast.9, bf16[4096,128]{1,0:T(8,128)(2,1)} %get-tuple-element.25.zn_cells, bf16[512,4096]{1,0:T(8,128)(2,1)} %get-tuple-element.23.factors, f32[128,128]{1,0:T(8,128)} %get-tuple-element.26.grad_gate, f32[128,128]{1,0:T(8,128)} %get-tuple-element.27.grad_out), custom_call_target="tpu_custom_call" | custom-call | flops 1000000000 | bytes 10000000 | tf_op jit(solution)/shard_map/pallas_call | solution.py:439
  137.9 14.7 %all_to_all.32.got = bf16[64,16,128]{2,1,0:T(8,128)(2,1)S(1)} all-to-all(bf16[64,16,128]{2,1,0:T(8,128)(2,1)} %shard_map.161), channel_id=1, replica_groups=mesh['row'=8,'col'=8,'rep'=2] {'row','col'}, dimensions={0} | all-to-all | bytes 524288 | tf_op jit(solution)/shard_map/all_to_all | solution.py:353
  152.5 0.8 shard_map.162
  153.3 4.5 %all-to-all-start.5 = ((bf16[64,16,128]{2,1,0:T(8,128)(2,1)}), bf16[64,16,128]{2,1,0:T(8,128)(2,1)S(1)}, u32[]{:S(2)}, u32[]{:S(2)}) async-start(bf16[64,16,128]{2,1,0:T(8,128)(2,1)} %shard_map.162), calls=%async_computation.5 | async-start | bytes 524288 | tf_op jit(solution)/shard_map/all_to_all | solution.py:353
  157.9 7.1 %shard_map.160 = bf16[64,64,128]{2,1,0:T(8,128)(2,1)} custom-call(bf16[64,64,128]{2,1,0:T(8,128)(2,1)} %pair.3, f32[1,128]{1,0:T(1,128)S(1)} %bitcast.15, bf16[64,2,64,128]{3,2,1,0:T(8,128)(2,1)S(1)} %bitcast.10, bf16[512,4096]{1,0:T(8,128)(2,1)} %get-tuple-element.23.factors, bf16[128,4096]{1,0:T(8,128)(2,1)} %get-tuple-element.24.dg, ...), custom_call_target="tpu_custom_call" | custom-call | flops 1000000000 | bytes 10000000 | tf_op jit(solution)/shard_map/pallas_call | solution.py:448
  165.0 2.5 %all-to-all-done.5.got = bf16[64,16,128]{2,1,0:T(8,128)(2,1)S(1)} async-done(((bf16[64,16,128]{2,1,0:T(8,128)(2,1)}), bf16[64,16,128]{2,1,0:T(8,128)(2,1)S(1)}, u32[]{:S(2)}, u32[]{:S(2)}) %all-to-all-start.5) | async-done | bytes 262176 | tf_op jit(solution)/shard_map/all_to_all | solution.py:353
  167.5 0.9 shard_map.163
  (5 shorter events, 0.0 us)
Async XLA Ops:
  1.3 0.7 copy-start
  1.9 0.7 copy-start.2
  45.9 7.3 %copy-start.3 = (f32[128]{0:T(128)S(1)}, f32[128]{0:T(128)}, u32[]{:S(2)}) copy-start(f32[128]{0:T(128)} %param.18) | copy-start | bytes 1540
  48.2 22.9 %all-to-all-start.1 = ((bf16[64,64,128]{2,1,0:T(8,128)(2,1)}), bf16[64,64,128]{2,1,0:T(8,128)(2,1)S(1)}, u32[]{:S(2)}, u32[]{:S(2)}) async-start(bf16[64,64,128]{2,1,0:T(8,128)(2,1)} %bitcast.21), calls=%async_computation.1 | async-start | bytes 2097152 | tf_op jit(solution)/shard_map/all_to_all | solution.py:353
  99.9 4.5 %copy-start.4 = (f32[128]{0:T(128)S(1)}, f32[128]{0:T(128)}, u32[]{:S(2)}) copy-start(f32[128]{0:T(128)} %param.19) | copy-start | bytes 1540
  99.9 32.9 %all-to-all-start.3 = ((bf16[64,128,128]{2,1,0:T(8,128)(2,1)}), bf16[64,128,128]{2,1,0:T(8,128)(2,1)S(1)}, u32[]{:S(2)}, u32[]{:S(2)}) async-start(bf16[64,128,128]{2,1,0:T(8,128)(2,1)} %bitcast.20), calls=%async_computation.3 | async-start | bytes 4194304 | tf_op jit(solution)/shard_map/all_to_all | solution.py:353
  132.9 25.0 %copy-start.1 = (f32[128]{0:T(128)S(1)}, f32[128]{0:T(128)}, u32[]{:S(2)}) copy-start(f32[128]{0:T(128)} %param.13) | copy-start | bytes 1540
  153.3 14.2 %all-to-all-start.5 = ((bf16[64,16,128]{2,1,0:T(8,128)(2,1)}), bf16[64,16,128]{2,1,0:T(8,128)(2,1)S(1)}, u32[]{:S(2)}, u32[]{:S(2)}) async-start(bf16[64,16,128]{2,1,0:T(8,128)(2,1)} %shard_map.162), calls=%async_computation.5 | async-start | bytes 524288 | tf_op jit(solution)/shard_map/all_to_all | solution.py:353

commit v7 on v6

--- a/solution.py
+++ b/solution.py
@@ -225,9 +225,11 @@
 
 
 def product_grads_kernel(got, operands_ref, send, a_scr, b_scr, d_scr, out_scr, sems):
-    def copy(which):
-        part = (slice(None), which)
-        return pltpu.make_async_copy(out_scr.at[part], send.at[part], sems.at[which])
+    def copy(which, first, count, sem):
+        part = (pl.ds(first, count), which)
+        return pltpu.make_async_copy(out_scr.at[part], send.at[part], sems.at[sem])
+
+    copies = [copy(0, 0, 64, 0), copy(1, 0, 32, 1), copy(1, 32, 32, 2)]
 
     gather_map(operands_ref, 0, a_scr)
     double_rows(operands_ref, 1, b_scr)
@@ -239,7 +241,7 @@
         for r in range(8):
             for c in range(2):
                 out_scr[r * 8 + 2 * n + c, 0] = out[r * 64 : (r + 1) * 64, c * 128 : (c + 1) * 128]
-    copy(0).start()
+    copies[0].start()
     low = low_half((64, 128))
     for m in range(2):
         out = dot(d_scr[:, m * 512 : (m + 1) * 512], a_scr[...], 0, 0)
@@ -249,9 +251,9 @@
                 out_scr[(m * 4 + r) * 8 + c, 1] = jnp.where(
                     low, out[r * 128 : r * 128 + 64, lanes], out[r * 128 + 64 : (r + 1) * 128, lanes]
                 ).astype(BF)
-    copy(1).start()
-    copy(0).wait()
-    copy(1).wait()
+        copies[1 + m].start()
+    for started in copies:
+        started.wait()
 
 
 def cell_grads(got, which, factors, scr):
@@ -432,7 +434,7 @@
         [direct, direct],
         pl.BlockSpec(memory_space=pltpu.HBM),
         shape((64, 2, 64, 128), BF, far),
-        [a_map, b_map, a_map, pltpu.VMEM((64, 2, 64, 128), BF), pltpu.SemaphoreType.DMA((2,))],
+        [a_map, b_map, a_map, pltpu.VMEM((64, 2, 64, 128), BF), pltpu.SemaphoreType.DMA((3,))],
     )(keep(got, near), operands)
 
     grads = keep(exchange(send), near)

time: 169 us -> 169 us (level)
  no operation moved by 1% of the time
where the time goes in v7:
time: 169 us; the launch traced here: 168 us
  blocking collectives  76.1 us (45%)
  Pallas kernels  38.6 us (23%)
  waiting for transfers between devices  36.9 us (22%)
  starting transfers between devices  14 us (8%)
    all_to_all x3, blocking collectives, exchange(): return lax.all_to_all(flat, AXES, 0, 0, tiled=True).reshape(values.shape)  76.1 us
    all_to_all x3, waiting for transfers between devices, exchange(): return lax.all_to_all(flat, AXES, 0, 0, tiled=True).reshape(values.shape)  36.9 us
    all_to_all x3, starting transfers between devices, exchange(): return lax.all_to_all(flat, AXES, 0, 0, tiled=True).reshape(values.shape)  14 us
    pallas_call x1, Pallas kernels, body(): call(pair_kernel, grid, [natural, vec, direct, chan_major4, chan_major] +...  7.13 us
    pallas_call x1, Pallas kernels, body(): call(factors_kernel, grid, [chan_major, scalar, natural, vec, wide, wide,...  6.98 us
    pallas_call x1, Pallas kernels, body(): call(updated_kernel, grid, [single, chan_major, natural, vec, vec, square...  5.06 us
    pallas_call x1, Pallas kernels, body(): call(weights_kernel, grid, [direct, cell_major, chan_major4] + [square, s...  4.98 us
    pallas_call x1, Pallas kernels, body(): call(operands_kernel, grid, [natural, scalar, vec, vec, wide, wide], [dir...  4.11 us
  transfers between devices with their start and end apart: 3, of which 3 were waited for; matrix products, arithmetic and copies ran while one was open for 0% of the time, Pallas kernels for 11%

profile of v7, /device:TPU:1, one launch (start us, length us, event | category | flops | bytes accessed | tf_op | source)
XLA Modules:
  0.0 168.2 jit_solution(12729734812447447561)
XLA Ops:
  1.3 0.0 copy-start
  1.3 0.6 copy-done
  1.9 0.7 copy-done.2
  2.6 4.1 %shard_map.154 = (bf16[64,2,64,128]{3,2,1,0:T(8,128)(2,1)S(1)}, bf16[128,4096]{1,0:T(8,128)(2,1)}) custom-call(bf16[64,64,128]{2,1,0:T(8,128)(2,1)} %pair.3, s32[1]{0:T(128)S(6)} %copy.17.length, f32[1,128]{1,0:T(1,128)S(1)} %bitcast.14, f32[1,128]{1,0:T(1,128)S(1)} %bitcast.16, bf16[128,256]{1,0:T(8,128)(2,1)} %w_left.5, bf16[128,256]{1,0:T(8,128)(2,1)} %w_right.5), custom_call_target="tpu_custom_call" | custom-call | flops 1000000000 | bytes 10000000 | tf_op jit(solution)/shard_map/pallas_call | solution.py:388
  6.7 39.2 %all_to_all.30 = bf16[64,128,128]{2,1,0:T(8,128)(2,1)S(1)} all-to-all(bf16[64,128,128]{2,1,0:T(8,128)(2,1)S(1)} %bitcast.13), channel_id=1, replica_groups=mesh['row'=8,'col'=8,'rep'=2] {'row','col'}, dimensions={0} | all-to-all | bytes 4194304 | tf_op jit(solution)/shard_map/all_to_all | solution.py:355
  45.9 2.3 %shard_map.155 = bf16[8,8,64,128]{3,2,1,0:T(8,128)(2,1)} custom-call(bf16[64,2,64,128]{3,2,1,0:T(8,128)(2,1)S(1)} %bitcast.11), custom_call_target="tpu_custom_call" | custom-call | flops 1000000000 | bytes 10000000 | tf_op jit(solution)/shard_map/pallas_call | solution.py:407
  48.2 5.0 %all-to-all-start.1 = ((bf16[64,64,128]{2,1,0:T(8,128)(2,1)}), bf16[64,64,128]{2,1,0:T(8,128)(2,1)S(1)}, u32[]{:S(2)}, u32[]{:S(2)}) async-start(bf16[64,64,128]{2,1,0:T(8,128)(2,1)} %bitcast.21), calls=%async_computation.1 | async-start | bytes 2097152 | tf_op jit(solution)/shard_map/all_to_all | solution.py:355
  53.2 7.0 %shard_map.157 = (bf16[512,4096]{1,0:T(8,128)(2,1)}, f32[64,64,128]{2,1,0:T(8,128)}, bf16[4096,128]{1,0:T(8,128)(2,1)}) custom-call(bf16[128,4096]{1,0:T(8,128)(2,1)} %get-tuple-element.20.zn_ref, s32[1]{0:T(128)S(6)} %copy.17.length, bf16[64,64,128]{2,1,0:T(8,128)(2,1)} %cot.3, f32[1,128]{1,0:T(1,128)S(1)} %bitcast.17, bf16[128,256]{1,0:T(8,128)(2,1)} %w_left.5, ...), custom_call_target="tpu_custom_call" | custom-call | flops 1000000000 | bytes 10000000 | tf_op jit(solution)/shard_map/pallas_call | solution.py:398
  60.2 11.0 %all-to-all-done.1.product.got = bf16[64,64,128]{2,1,0:T(8,128)(2,1)S(1)} async-done(((bf16[64,64,128]{2,1,0:T(8,128)(2,1)}), bf16[64,64,128]{2,1,0:T(8,128)(2,1)S(1)}, u32[]{:S(2)}, u32[]{:S(2)}) %all-to-all-start.1) | async-done | bytes 1048608 | tf_op jit(solution)/shard_map/all_to_all | solution.py:355
  71.2 2.9 %shard_map.158 = bf16[64,64,128]{2,1,0:T(8,128)(2,1)S(1)} custom-call(bf16[64,64,128]{2,1,0:T(8,128)(2,1)S(1)} %all-to-all-done.1.product.got, f32[64,64,128]{2,1,0:T(8,128)} %get-tuple-element.22.hat_grad), custom_call_target="tpu_custom_call" | custom-call | flops 1000000000 | bytes 10000000 | tf_op jit(solution)/shard_map/pallas_call | solution.py:416
  74.0 22.2 %all_to_all.31.got = bf16[64,64,128]{2,1,0:T(8,128)(2,1)S(1)} all-to-all(bf16[64,64,128]{2,1,0:T(8,128)(2,1)S(1)} %shard_map.158), channel_id=1, replica_groups=mesh['row'=8,'col'=8,'rep'=2] {'row','col'}, dimensions={0} | all-to-all | bytes 2097152 | tf_op jit(solution)/shard_map/all_to_all | solution.py:355
  96.2 3.5 %shard_map.159 = bf16[64,2,64,128]{3,2,1,0:T(8,128)(2,1)} custom-call(bf16[64,64,128]{2,1,0:T(8,128)(2,1)S(1)} %all_to_all.31.got, bf16[64,2,64,128]{3,2,1,0:T(8,128)(2,1)S(1)} %bitcast.12), custom_call_target="tpu_custom_call" | custom-call | flops 1000000000 | bytes 10000000 | tf_op jit(solution)/shard_map/pallas_call | solution.py:432
  99.7 0.0 copy-start.4
  99.7 4.5 %all-to-all-start.3 = ((bf16[64,128,128]{2,1,0:T(8,128)(2,1)}), bf16[64,128,128]{2,1,0:T(8,128)(2,1)S(1)}, u32[]{:S(2)}, u32[]{:S(2)}) async-start(bf16[64,128,128]{2,1,0:T(8,128)(2,1)} %bitcast.20), calls=%async_computation.3 | async-start | bytes 4194304 | tf_op jit(solution)/shard_map/all_to_all | solution.py:355
  104.2 5.1 %shard_map.156 = (bf16[64,64,128]{2,1,0:T(8,128)(2,1)}, bf16[128,4096]{1,0:T(8,128)(2,1)}, f32[128,128]{1,0:T(8,128)}, f32[128,128]{1,0:T(8,128)}) custom-call(bf16[64,64,128]{2,1,0:T(8,128)(2,1)S(1)} %all-to-all-done.1.product.got, bf16[128,4096]{1,0:T(8,128)(2,1)} %get-tuple-element.20.zn_ref, bf16[64,64,128]{2,1,0:T(8,128)(2,1)} %cot.3, ...), custom_call_target="tpu_custom_call" | custom-call | flops 1000000000 | bytes 10000000 | tf_op jit(solution)/shard_map/pallas_call | solution.py:424
  109.3 23.4 %all-to-all-done.3 = bf16[64,128,128]{2,1,0:T(8,128)(2,1)S(1)} async-done(((bf16[64,128,128]{2,1,0:T(8,128)(2,1)}), bf16[64,128,128]{2,1,0:T(8,128)(2,1)S(1)}, u32[]{:S(2)}, u32[]{:S(2)}) %all-to-all-start.3) | async-done | bytes 2097184 | tf_op jit(solution)/shard_map/all_to_all | solution.py:355
  132.7 5.0 %shard_map.161 = bf16[64,16,128]{2,1,0:T(8,128)(2,1)} custom-call(bf16[64,2,64,128]{3,2,1,0:T(8,128)(2,1)S(1)} %bitcast.9, bf16[4096,128]{1,0:T(8,128)(2,1)} %get-tuple-element.25.zn_cells, bf16[512,4096]{1,0:T(8,128)(2,1)} %get-tuple-element.23.factors, f32[128,128]{1,0:T(8,128)} %get-tuple-element.26.grad_gate, f32[128,128]{1,0:T(8,128)} %get-tuple-element.27.grad_out), custom_call_target="tpu_custom_call" | custom-call | flops 1000000000 | bytes 10000000 | tf_op jit(solution)/shard_map/pallas_call | solution.py:441
  137.7 14.7 %all_to_all.32.got = bf16[64,16,128]{2,1,0:T(8,128)(2,1)S(1)} all-to-all(bf16[64,16,128]{2,1,0:T(8,128)(2,1)} %shard_map.161), channel_id=1, replica_groups=mesh['row'=8,'col'=8,'rep'=2] {'row','col'}, dimensions={0} | all-to-all | bytes 524288 | tf_op jit(solution)/shard_map/all_to_all | solution.py:355
  152.3 0.8 shard_map.162
  153.1 4.5 %all-to-all-start.5 = ((bf16[64,16,128]{2,1,0:T(8,128)(2,1)}), bf16[64,16,128]{2,1,0:T(8,128)(2,1)S(1)}, u32[]{:S(2)}, u32[]{:S(2)}) async-start(bf16[64,16,128]{2,1,0:T(8,128)(2,1)} %shard_map.162), calls=%async_computation.5 | async-start | bytes 524288 | tf_op jit(solution)/shard_map/all_to_all | solution.py:355
  157.7 0.0 copy-done.1
  157.7 7.1 %shard_map.160 = bf16[64,64,128]{2,1,0:T(8,128)(2,1)} custom-call(bf16[64,64,128]{2,1,0:T(8,128)(2,1)} %pair.3, f32[1,128]{1,0:T(1,128)S(1)} %bitcast.15, bf16[64,2,64,128]{3,2,1,0:T(8,128)(2,1)S(1)} %bitcast.10, bf16[512,4096]{1,0:T(8,128)(2,1)} %get-tuple-element.23.factors, bf16[128,4096]{1,0:T(8,128)(2,1)} %get-tuple-element.24.dg, ...), custom_call_target="tpu_custom_call" | custom-call | flops 1000000000 | bytes 10000000 | tf_op jit(solution)/shard_map/pallas_call | solution.py:450
  164.8 2.5 %all-to-all-done.5.got = bf16[64,16,128]{2,1,0:T(8,128)(2,1)S(1)} async-done(((bf16[64,16,128]{2,1,0:T(8,128)(2,1)}), bf16[64,16,128]{2,1,0:T(8,128)(2,1)S(1)}, u32[]{:S(2)}, u32[]{:S(2)}) %all-to-all-start.5) | async-done | bytes 262176 | tf_op jit(solution)/shard_map/all_to_all | solution.py:355
  167.3 0.9 shard_map.163
  (5 shorter events, 0.0 us)
Async XLA Ops:
  1.3 0.7 copy-start
  1.9 0.7 copy-start.2
  45.9 7.3 %copy-start.3 = (f32[128]{0:T(128)S(1)}, f32[128]{0:T(128)}, u32[]{:S(2)}) copy-start(f32[128]{0:T(128)} %param.18) | copy-start | bytes 1540
  48.2 22.9 %all-to-all-start.1 = ((bf16[64,64,128]{2,1,0:T(8,128)(2,1)}), bf16[64,64,128]{2,1,0:T(8,128)(2,1)S(1)}, u32[]{:S(2)}, u32[]{:S(2)}) async-start(bf16[64,64,128]{2,1,0:T(8,128)(2,1)} %bitcast.21), calls=%async_computation.1 | async-start | bytes 2097152 | tf_op jit(solution)/shard_map/all_to_all | solution.py:355
  99.7 4.5 %copy-start.4 = (f32[128]{0:T(128)S(1)}, f32[128]{0:T(128)}, u32[]{:S(2)}) copy-start(f32[128]{0:T(128)} %param.19) | copy-start | bytes 1540
  99.7 32.9 %all-to-all-start.3 = ((bf16[64,128,128]{2,1,0:T(8,128)(2,1)}), bf16[64,128,128]{2,1,0:T(8,128)(2,1)S(1)}, u32[]{:S(2)}, u32[]{:S(2)}) async-start(bf16[64,128,128]{2,1,0:T(8,128)(2,1)} %bitcast.20), calls=%async_computation.3 | async-start | bytes 4194304 | tf_op jit(solution)/shard_map/all_to_all | solution.py:355
  132.7 25.0 %copy-start.1 = (f32[128]{0:T(128)S(1)}, f32[128]{0:T(128)}, u32[]{:S(2)}) copy-start(f32[128]{0:T(128)} %param.13) | copy-start | bytes 1540
  153.1 14.2 %all-to-all-start.5 = ((bf16[64,16,128]{2,1,0:T(8,128)(2,1)}), bf16[64,16,128]{2,1,0:T(8,128)(2,1)S(1)}, u32[]{:S(2)}, u32[]{:S(2)}) async-start(bf16[64,16,128]{2,1,0:T(8,128)(2,1)} %shard_map.162), calls=%async_computation.5 | async-start | bytes 524288 | tf_op jit(solution)/shard_map/all_to_all | solution.py:355
